TPU v7x, 32 devices: a whole 2x2x4 slice. The times are simulated.
32 devices in a mesh: section: 4 (over x, core), cls: 8 (over z, y).
Axes of the slice: x: 2, y: 2, z: 4, core: 2. Of those that a mesh axis runs over, the one named last changes fastest.
Arguments:
- images: bfloat16 [512, 256, 256], P(('section', 'cls')), may hold values from -6 to 6
- group_ids: int32 [512], P(('section', 'cls')), may hold values from 0 to 3
- row_filters: bfloat16 [4, 256, 256], replicated, may hold values from -0.375 to 0.375
- column_filters: bfloat16 [4, 256, 256], replicated, may hold values from -0.375 to 0.375
- basis_rows: bfloat16 [256, 16], replicated, may hold values from -0.375 to 0.375
- basis_columns: bfloat16 [256, 16], replicated, may hold values from -0.375 to 0.375
- rotations: bfloat16 [36, 256, 256], P('section'), may hold values from -0.375 to 0.375
- references: bfloat16 [16, 256], P('cls'), may hold values from -2 to 2
- sharpness: bfloat16 [512], P(('section', 'cls')), may hold values from 0.049804688 to 2
- best_rotation: int32 [512], P(('section', 'cls')), may hold values from 0 to 35
- assignments: int32 [512, 16], P(('section', 'cls')), may hold values from 0 to 15, all different within a row; in each aligned block of 16 rows (0 to 15, 16 to 31, ...) at most 16 rows name the same one
Outputs:
- new_references: float32 [16, 256], P('cls')
- evidence: float32 [512], P(('section', 'cls'))
Inputs may be any that keep to these rules, and one draw needn't show every extreme that they name: `assignments`: each particle lists 16 different classes; among the particles of one device no class is listed more than 16 times, a bound that some block reaches.
All inputs are finite; a program needn't handle non-finite values.
Results may differ from a plain program's by a relative error of at most 0.019.
Values may be sent and summed in bfloat16 or wider, within the bound.
No kernel may reach another device: no remote copies, remote signals or barrier semaphores. Data moves between devices by JAX's collectives and lax.ppermute only.
A program may use at most 64 MiB of HBM per device.

v0:
```python
import math

import jax
import jax.numpy as jnp
from jax import lax
from jax.sharding import PartitionSpec as P

EPSILON = 1e-05


def soft_edge(pixels):
    coordinate = (jnp.arange(pixels, dtype=jnp.float32) - (pixels - 1) / 2.0) / (pixels / 2.0)
    radius = jnp.sqrt(
        coordinate[:, None] * coordinate[:, None] + coordinate[None, :] * coordinate[None, :]
    )
    falloff = jnp.clip((radius - 0.8) / 0.15, 0.0, 1.0)
    return 0.5 + 0.5 * jnp.cos(math.pi * falloff)


def filter_images(images, group_ids, row_filters, column_filters, basis_rows, basis_columns):
    column_each = jnp.take(column_filters, group_ids, axis=0)
    row_each = jnp.take(row_filters, group_ids, axis=0)
    filtered_half = jnp.einsum(
        "bij,bjk->bik", images, column_each, preferred_element_type=jnp.float32
    ).astype(jnp.bfloat16)
    filtered = jnp.einsum(
        "bij,bjk->bik", row_each, filtered_half, preferred_element_type=jnp.float32
    )
    masked = filtered * soft_edge(images.shape[1])
    power = jnp.mean(masked * masked, axis=(1, 2), keepdims=True)
    normed = (masked * lax.rsqrt(power + EPSILON)).astype(jnp.bfloat16)
    inner = jnp.einsum("bij,jk->bik", normed, basis_columns, preferred_element_type=jnp.float32)
    coeffs = jnp.einsum(
        "ja,bjk->bak", basis_rows.astype(jnp.float32), inner, precision=lax.Precision.HIGHEST
    )
    return coeffs.reshape(coeffs.shape[0], -1).astype(jnp.bfloat16)


def body(
    images,
    group_ids,
    row_filters,
    column_filters,
    basis_rows,
    basis_columns,
    rotations,
    references,
    sharpness,
    best_rotation,
    assignments,
):
    particles = images.shape[0]
    listed = assignments.shape[1]
    coeffs = filter_images(
        images, group_ids, row_filters, column_filters, basis_rows, basis_columns
    )
    gathered, gathered_sharp = (
        lax.all_gather(coeffs, "section", axis=0, tiled=True),
        lax.all_gather(sharpness, "section", axis=0, tiled=True),
    )
    gathered_best = lax.all_gather(best_rotation, "section", axis=0, tiled=True)
    all_refs = lax.all_gather(references, "cls", axis=0, tiled=True)
    classes = all_refs.shape[0]
    width = all_refs.shape[1]
    sections = lax.axis_size("section")
    local_rotations = rotations.shape[0]
    first_rotation = lax.axis_index("section") * local_rotations
    turned = jnp.einsum(
        "rkl,nl->nrk", rotations, gathered, preferred_element_type=jnp.float32
    ).astype(jnp.bfloat16)
    products = jnp.einsum("nrk,ck->nrc", turned, all_refs, preferred_element_type=jnp.float32)
    scores = products * gathered_sharp.astype(jnp.float32)[:, None, None]
    maxima = jnp.max(scores, axis=1)
    totals = jnp.sum(jnp.exp(scores - maxima[:, None, :]), axis=1)
    partial_marg = (maxima + jnp.log(totals)).reshape(sections, particles, classes)
    received_marg = lax.all_to_all(partial_marg, "section", split_axis=0, concat_axis=0, tiled=True)
    own_marg = jax.nn.logsumexp(received_marg, axis=0)
    evidence = jax.nn.logsumexp(own_marg, axis=1)
    class_range = jnp.arange(classes, dtype=jnp.int32)
    matches = assignments[:, :, None] == class_range[None, None, :]
    picked = jnp.sum(jnp.where(matches, own_marg[:, None, :], 0.0), axis=2)
    weights = jax.nn.softmax(picked, axis=1).astype(jnp.bfloat16)
    offset = gathered_best - first_rotation
    chosen = (offset[:, None] == jnp.arange(local_rotations, dtype=jnp.int32)[None, :]).astype(
        jnp.bfloat16
    )
    partial_rows = jnp.einsum("nrk,nr->nk", turned, chosen, preferred_element_type=jnp.float32)
    aligned = lax.psum_scatter(
        partial_rows.astype(jnp.bfloat16), "section", scatter_dimension=0, tiled=True
    )
    contribution = (
        weights.astype(jnp.float32)[:, :, None] * aligned.astype(jnp.float32)[:, None, :]
    ).astype(jnp.bfloat16)
    flat_classes = assignments.reshape(-1)
    flat_contribution = contribution.reshape(-1, width)
    flat_weights = weights.reshape(-1)
    owners = lax.axis_size("cls")
    own_classes = references.shape[0]
    capacity = max(2, -(-(particles * listed) // classes))
    onehot = (flat_classes[:, None] == class_range[None, :]).astype(jnp.int32)
    slot_rank = jnp.sum((jnp.cumsum(onehot, axis=0) - 1) * onehot, axis=1)
    slot_index = flat_classes * capacity + slot_rank
    buffer = (
        jnp.zeros((classes * capacity, width), jnp.bfloat16).at[slot_index].set(flat_contribution)
    )
    weight_slots = jnp.zeros((classes * capacity,), jnp.bfloat16).at[slot_index].set(flat_weights)
    buffer = buffer.reshape(owners, own_classes, capacity, width)
    weight_slots = weight_slots.reshape(owners, own_classes, capacity)
    received, received_weights = (
        lax.all_to_all(buffer, "cls", split_axis=0, concat_axis=0, tiled=True),
        lax.all_to_all(weight_slots, "cls", split_axis=0, concat_axis=0, tiled=True),
    )
    class_sums = jnp.sum(received.astype(jnp.float32), axis=(0, 2))
    class_weights = jnp.sum(received_weights.astype(jnp.float32), axis=(0, 2))
    class_sums, class_weights = lax.psum((class_sums, class_weights), "section")
    new_references = (class_sums + references.astype(jnp.float32)) / (class_weights[:, None] + 1.0)
    return (new_references, evidence)


def solution(mesh):
    in_specs = (
        P(("section", "cls"), None, None),
        P(("section", "cls")),
        P(),
        P(),
        P(),
        P(),
        P("section", None, None),
        P("cls", None),
        P(("section", "cls")),
        P(("section", "cls")),
        P(("section", "cls"), None),
    )
    out_specs = (P("cls", None), P(("section", "cls")))
    return jax.shard_map(body, mesh=mesh, in_specs=in_specs, out_specs=out_specs, check_vma=False)
```

profile of v0, /device:TPU:0, one launch (start us, length us, event | category | flops | bytes accessed | tf_op | source)
XLA Modules:
  0.0 119.3 jit_solution(8362386343896583370)
XLA Ops:
  7.2 0.8 compare_select_fusion.1
  8.7 3.1 %gather_fusion = bf16[16,256,256]{2,1,0:T(8,128)(2,1)} fusion(bf16[4,256,256]{2,1,0:T(8,128)(2,1)} %param.15, s32[1024]{0:T(1024)S(1)} %pad_clamp_fusion), kind=kCustom, calls=%fused_computation.clone | custom fusion | bytes 4194368 | tf_op jit(solution)/shard_map/jit(_take)/gather | solution.py:22
  11.8 2.0 %gather_fusion.1 = bf16[16,256,256]{2,1,0:T(8,128)(2,1)} fusion(bf16[4,256,256]{2,1,0:T(8,128)(2,1)S(1)} %copy-done.1, s32[1024]{0:T(1024)S(1)} %pad_clamp_fusion), kind=kCustom, calls=%fused_computation.1.clone | custom fusion | bytes 4194368 | tf_op jit(solution)/shard_map/jit(_take)/gather | solution.py:21
  13.8 1.0 multiply_add_fusion
  14.9 5.7 %multiply_reduce_fusion = (f32[16]{0:T(128)S(1)}, f32[16,256,256]{2,1,0:T(8,128)}) fusion(f32[256,256]{1,0:T(8,128)S(1)} %multiply_add_fusion, bf16[16,256,256]{2,1,0:T(8,128)(2,1)S(1)} %copy-done, bf16[16,256,256]{2,1,0:T(8,128)(2,1)} %gather_fusion.1, pred[16]{0:T(512)(128)(4,1)S(1)} %compare_and_fusion, bf16[16,256,256]{2,1,0:T(8,128)(2,1)} %gather_fusion), kind=kOutput, calls=%fused_computation.5 | convolution fusion | flops 1080033280 | bytes 10747984 | tf_op jit(solution)/shard_map/bij,bjk->bik/dot_general | solution.py:26
  20.6 3.0 %fusion = f32[16,256,16]{1,2,0:T(8,128)S(1)} fusion(f32[16,256,256]{2,1,0:T(8,128)} %get-tuple-element.8, f32[16]{0:T(128)S(1)} %add_rsqrt_fusion, f32[256,256]{1,0:T(8,128)S(1)} %multiply_add_fusion, bf16[256,16]{0,1:T(8,128)(2,1)S(1)} %copy-done.5), kind=kOutput, calls=%fused_computation.6 | convolution fusion | flops 36700160 | bytes 4726848 | tf_op jit(solution)/shard_map/bij,jk->bik/dot_general | solution.py:32
  24.1 6.2 %all_gather.12 = bf16[64,256]{1,0:T(8,128)(2,1)S(1)} all-gather(bf16[16,256]{1,0:T(8,128)(2,1)S(1)} %convert_element_type.71), channel_id=1, replica_groups=mesh['section'=4,'cls'=8] {'section'}, dimensions={0}, use_global_device_ids=true | all-gather | bytes 40960 | tf_op jit(solution)/shard_map/all_gather | solution.py:58
  30.3 1.2 %dynamic-slice = u32[1]{0:T(128)} dynamic-slice(u32[32]{0:T(128)} %constant.75, u32[]{:T(128)S(6)} %add.117), dynamic_slice_sizes={1} | dynamic-slice | bytes 12
  32.5 7.5 %all-reduce = bf16[64]{0:T(256)(128)(2,1)S(1)} all-reduce(bf16[64]{0:T(256)(128)(2,1)S(1)} %dynamic-update-slice), channel_id=1, replica_groups=mesh['section'=4,'cls'=8] {'section'}, use_global_device_ids=true, to_apply=%add | all-reduce | flops 64 | bytes 256
  40.0 20.8 %all-gather = bf16[8,2,256]{2,1,0:T(2,128)(2,1)S(1)} all-gather(bf16[1,2,256]{2,1,0:T(2,128)(2,1)S(1)} %bitcast.56), channel_id=1, replica_groups=mesh['section'=4,'cls'=8] {'cls'}, dimensions={0}, use_global_device_ids=true | all-gather | bytes 9216 | tf_op jit(solution)/shard_map/all_gather | solution.py:62
  61.3 0.7 copy-done.3
  62.4 0.7 reshape.260
  63.1 3.2 %all-to-all-start = ((f32[4,1,256]{2,1,0:T(1,128)}), f32[4,1,256]{2,1,0:T(1,128)S(1)}, u32[]{:S(2)}, u32[]{:S(2)}) async-start(f32[4,1,256]{2,1,0:T(1,128)} %reshape.260), calls=%async_computation | async-start | bytes 8192 | tf_op jit(solution)/shard_map/all_to_all | solution.py:76
  66.6 5.3 %all-reduce.1 = s32[64]{0:T(128)S(1)} all-reduce(s32[64]{0:T(128)S(1)} %dynamic-update-slice.1), channel_id=1, replica_groups=mesh['section'=4,'cls'=8] {'section'}, use_global_device_ids=true, to_apply=%add.1 | all-reduce | flops 64 | bytes 512
  72.0 1.3 %fusion.17 = bf16[64,1,256]{2,1,0:T(2,128)(2,1)S(1)} fusion(bf16[64,9,256]{2,0,1:T(8,128)(2,1)} %copy-done.3, pred[64,9,1]{1,0,2:T(32,128)(4,1)S(1)} %fusion.24), kind=kOutput, calls=%fused_computation.21 | convolution fusion | flops 294912 | bytes 328256 | tf_op jit(solution)/shard_map/nrk,nr->nk/dot_general | solution.py:87
  77.2 2.2 %scatter_custom_fusion.1 = bf16[256]{0:T(256)(128)(2,1)S(1)} fusion(s32[256]{0:T(256)S(1)} %bitcast.57, bf16[256]{0:T(256)(128)(2,1)S(1)} %reshape.226, bf16[]{:T(256)} %constant.26.clone.1), kind=kCustom, calls=%fused_computation.67 | custom fusion | bytes 514 | tf_op jit(solution)/shard_map/scatter | solution.py:106
  79.4 0.7 reshape.197
  80.1 3.2 %all-to-all-start.2 = ((bf16[8,2,16]{2,1,0:T(2,128)(2,1)}), bf16[8,2,16]{2,1,0:T(2,128)(2,1)S(1)}, u32[]{:S(2)}, u32[]{:S(2)}) async-start(bf16[8,2,16]{2,1,0:T(2,128)(2,1)} %reshape.197), calls=%async_computation.3 | async-start | bytes 8192 | tf_op jit(solution)/shard_map/all_to_all | solution.py:111
  83.4 6.7 %reduce-scatter.2.cloned.1.call-done = bf16[16,256]{1,0:T(8,128)(2,1)} async-done(((bf16[64,256]{1,0:T(8,128)(2,1)}), bf16[16,256]{1,0:T(8,128)(2,1)}) %reduce-scatter.2.cloned.1.call-update) | async-done | bytes 8208 | tf_op jit(solution)/shard_map/reduce_scatter | solution.py:88
  90.1 0.7 convert_element_type.78
  90.9 2.1 %scatter_custom_fusion = bf16[256,256]{1,0:T(8,128)(2,1)} fusion(s32[256]{0:T(256)S(1)} %bitcast.58, bf16[256,256]{1,0:T(8,128)(2,1)S(1)} %fusion.19, bf16[]{:T(256)} %constant.26.clone.1), kind=kCustom, calls=%fused_computation.32 | custom fusion | bytes 131074 | tf_op jit(solution)/shard_map/scatter | solution.py:104
  93.0 5.5 %all-to-all-start.1 = ((bf16[8,2,16,256]{3,2,1,0:T(8,128)(2,1)}), bf16[8,2,16,256]{3,2,1,0:T(8,128)(2,1)S(1)}, u32[]{:S(2)}, u32[]{:S(2)}) async-start(bf16[8,2,16,256]{3,2,1,0:T(8,128)(2,1)} %bitcast.12), calls=%async_computation.2 | async-start | bytes 262144 | tf_op jit(solution)/shard_map/all_to_all | solution.py:110
  99.1 6.7 %all-to-all-done.1 = bf16[8,2,16,256]{3,2,1,0:T(8,128)(2,1)S(1)} async-done(((bf16[8,2,16,256]{3,2,1,0:T(8,128)(2,1)}), bf16[8,2,16,256]{3,2,1,0:T(8,128)(2,1)S(1)}, u32[]{:S(2)}, u32[]{:S(2)}) %all-to-all-start.1) | async-done | bytes 131104 | tf_op jit(solution)/shard_map/all_to_all | solution.py:110
  105.9 5.9 %all-reduce.2 = (f32[2,256]{1,0:T(2,128)S(1)}, f32[2]{0:T(128)S(1)}) all-reduce(f32[2,256]{1,0:T(2,128)S(1)} %convert_reduce_fusion, f32[2]{0:T(128)S(1)} %convert_reduce_fusion.1), channel_id=1, replica_groups=mesh['section'=4,'cls'=8] {'section'}, use_global_device_ids=true, to_apply=%region_14.16 | all-reduce | flops 514 | bytes 4112 | tf_op jit(solution)/shard_map/psum | solution.py:115
  (78 shorter events, 8.0 us)
Async XLA Ops:
  7.2 7.7 %copy-start = (bf16[16,256,256]{2,1,0:T(8,128)(2,1)S(1)}, bf16[16,256,256]{2,1,0:T(8,128)(2,1)}, u32[]{:S(2)}) copy-start(bf16[16,256,256]{2,1,0:T(8,128)(2,1)} %param.13) | copy-start | bytes 6291460
  8.7 3.1 %copy-start.1 = (bf16[4,256,256]{2,1,0:T(8,128)(2,1)S(1)}, bf16[4,256,256]{2,1,0:T(8,128)(2,1)}, u32[]{:S(2)}) copy-start(bf16[4,256,256]{2,1,0:T(8,128)(2,1)} %param.16) | copy-start | bytes 1572868
  14.9 5.7 %copy-start.5 = (bf16[256,16]{0,1:T(8,128)(2,1)S(1)}, bf16[256,16]{0,1:T(8,128)(2,1)}, u32[]{:S(2)}) copy-start(bf16[256,16]{0,1:T(8,128)(2,1)} %param.18) | copy-start | bytes 24580
  20.6 3.1 %copy-start.6 = (bf16[256,16]{0,1:T(8,128)(2,1)S(1)}, bf16[256,16]{0,1:T(8,128)(2,1)}, u32[]{:S(2)}) copy-start(bf16[256,16]{0,1:T(8,128)(2,1)} %param.17) | copy-start | bytes 24580
  20.6 11.6 %copy-start.8 = (bf16[16]{0:T(256)(128)(2,1)S(1)}, bf16[16]{0:T(256)(128)(2,1)}, u32[]{:S(2)}) copy-start(bf16[16]{0:T(256)(128)(2,1)} %param.21) | copy-start | bytes 100
  20.6 19.4 %copy-start.7 = (bf16[2,256]{1,0:T(2,128)(2,1)S(1)}, bf16[2,256]{1,0:T(2,128)(2,1)}, u32[]{:S(2)}) copy-start(bf16[2,256]{1,0:T(2,128)(2,1)} %param.20) | copy-start | bytes 3076
  20.6 40.2 %copy-start.2 = (bf16[9,256,256]{2,1,0:T(8,128)(2,1)S(1)}, bf16[9,256,256]{2,1,0:T(8,128)(2,1)}, u32[]{:S(2)}) copy-start(bf16[9,256,256]{2,1,0:T(8,128)(2,1)} %param.19) | copy-start | bytes 3538948
  23.6 42.8 %copy-start.9 = (s32[16]{0:T(128)S(1)}, s32[16]{0:T(128)}, u32[]{:S(2)}) copy-start(s32[16]{0:T(128)} %param.22) | copy-start | bytes 196
  23.6 50.3 %copy-start.4 = (s32[16,16]{1,0:T(8,128)S(1)}, s32[16,16]{1,0:T(8,128)}, u32[]{:S(2)}) copy-start(s32[16,16]{1,0:T(8,128)} %param.23) | copy-start | bytes 3076
  61.3 0.7 copy-start.3
  63.1 12.1 %all-to-all-start = ((f32[4,1,256]{2,1,0:T(1,128)}), f32[4,1,256]{2,1,0:T(1,128)S(1)}, u32[]{:S(2)}, u32[]{:S(2)}) async-start(f32[4,1,256]{2,1,0:T(1,128)} %reshape.260), calls=%async_computation | async-start | bytes 8192 | tf_op jit(solution)/shard_map/all_to_all | solution.py:76
  66.3 23.8 %reduce-scatter.2.cloned.1.call-start = ((), (), s32[]{:S(2)}) async-start(), calls=%async_computation.4 | async-start | bytes 40960 | tf_op jit(solution)/shard_map/reduce_scatter | solution.py:88
  80.1 12.9 %all-to-all-start.2 = ((bf16[8,2,16]{2,1,0:T(2,128)(2,1)}), bf16[8,2,16]{2,1,0:T(2,128)(2,1)S(1)}, u32[]{:S(2)}, u32[]{:S(2)}) async-start(bf16[8,2,16]{2,1,0:T(2,128)(2,1)} %reshape.197), calls=%async_computation.3 | async-start | bytes 8192 | tf_op jit(solution)/shard_map/all_to_all | solution.py:111
  93.0 12.9 %all-to-all-start.1 = ((bf16[8,2,16,256]{3,2,1,0:T(8,128)(2,1)}), bf16[8,2,16,256]{3,2,1,0:T(8,128)(2,1)S(1)}, u32[]{:S(2)}, u32[]{:S(2)}) async-start(bf16[8,2,16,256]{3,2,1,0:T(8,128)(2,1)} %bitcast.12), calls=%async_computation.2 | async-start | bytes 262144 | tf_op jit(solution)/shard_map/all_to_all | solution.py:110
Sparse Core Ops, SparseCore 0:
  74.1 15.9 reduce-scatter.1
where the time goes:
time: 120 us; the launch traced here: 119 us
  blocking collectives  45.8 us (38%)
  local copies, waits for them, and re-layouts  15.3 us (13%)
  between operations  15 us (12%)
  waiting for transfers between devices  13.5 us (11%)
  starting transfers between devices  12 us (10%)
  matrix products  10.9 us (9%)
  other arithmetic  6.83 us (6%)
    all_gather x1, blocking collectives, body(): all_refs = lax.all_gather(references, 'cls', axis=0, tiled=True)  20.8 us
    unnamed x2, blocking collectives  12.9 us
    all_to_all x1, waiting for transfers between devices, body(): lax.all_to_all(buffer, 'cls', split_axis=0, concat_axis=0, tiled=True)  6.72 us
    reduce_scatter x1, waiting for transfers between devices, body(): lax.psum_scatter(partial_rows.astype(jnp.bfloat16), 'section', scatter_di...  6.72 us
    all_gather x1, blocking collectives, body(): lax.all_gather(coeffs, 'section', axis=0, tiled=True)  6.17 us
    psum x1, blocking collectives, body(): class_sums, class_weights = lax.psum((class_sums, class_weights), 'section')  5.94 us
    dot_general x1, matrix products, filter_images(): jnp.einsum('bij,bjk->bik', row_each, filtered_half, preferred_element_typ...  5.67 us
    all_to_all x1, starting transfers between devices, body(): lax.all_to_all(buffer, 'cls', split_axis=0, concat_axis=0, tiled=True)  5.52 us
  transfers between devices with their start and end apart: 4, of which 2 were waited for; matrix products, arithmetic and copies ran while one was open for 10% of the time, Pallas kernels for 0%

commit v1 on v0

v1 whole, which is shorter than its diff:
```python
import math

import jax
import jax.numpy as jnp
import numpy as np
from jax import lax
from jax.experimental import pallas as pl
from jax.experimental.pallas import tpu as pltpu
from jax.sharding import PartitionSpec as P

EPSILON = 1e-05
LANES = 128
BF16 = jnp.bfloat16
F32 = jnp.float32


def soft_edge(pixels):
    coordinate = (np.arange(pixels, dtype=np.float32) - (pixels - 1) / 2.0) / (pixels / 2.0)
    radius = np.sqrt(coordinate[:, None] ** 2 + coordinate[None, :] ** 2)
    falloff = np.clip((radius - 0.8) / 0.15, 0.0, 1.0)
    return (0.5 + 0.5 * np.cos(math.pi * falloff)).astype(np.float32)


def filter_kernel(
    batch,
    own_classes,
    classes,
    groups_ref,
    best_ref,
    images_ref,
    row_ref,
    column_ref,
    mask_ref,
    basis_rows_ref,
    basis_columns_ref,
    assignments_ref,
    sharp_ref,
    out_ref,
    inner,
):
    step = pl.program_id(0)
    pixels = mask_ref.shape[0]
    row_count = basis_rows_ref.shape[0]
    column_count = basis_columns_ref.shape[0]
    width = row_count * column_count
    particles, message = out_ref.shape

    group = [groups_ref[step * batch + b] for b in range(batch)]
    half = [
        jnp.dot(images_ref[b], column_ref[group[b]], preferred_element_type=F32).astype(BF16)
        for b in range(batch)
    ]
    scale = []
    masked = []
    for b in range(batch):
        filtered = jnp.dot(row_ref[group[b]], half[b], preferred_element_type=F32) * mask_ref[...]
        power = jnp.sum(filtered * filtered, axis=0, keepdims=True)
        power = jnp.sum(power, axis=1, keepdims=True) * (1.0 / (pixels * pixels))
        scale.append(lax.rsqrt(power + EPSILON))
        masked.append(filtered.astype(BF16))
    for b in range(batch):
        rows = jnp.dot(basis_rows_ref[...], masked[b], preferred_element_type=F32)
        place = pl.multiple_of((step * batch + b) * row_count, row_count)
        inner[pl.ds(place, row_count), :] = rows * scale[b]

    @pl.when(step == pl.num_programs(0) - 1)
    def _():
        lane = lax.broadcasted_iota(jnp.int32, (column_count, width), 1)
        which = lax.broadcasted_iota(jnp.int32, (column_count, width), 0)
        spread = (lane % column_count == which).astype(F32).astype(BF16)
        wide = lax.dot_general(
            basis_columns_ref[...], spread, (((0,), (0,)), ((), ())), preferred_element_type=F32
        ).astype(BF16)
        held = inner[...]
        high = held.astype(BF16)
        low = (held - high.astype(F32)).astype(BF16)
        both = jnp.dot(high, wide, preferred_element_type=F32)
        both = both + jnp.dot(low, wide, preferred_element_type=F32)
        lane = lax.broadcasted_iota(jnp.int32, both.shape, 1)
        which = lax.broadcasted_iota(jnp.int32, both.shape, 0)
        both = jnp.where(lane // column_count == which % row_count, both, 0.0)
        coeffs = jnp.sum(both.reshape(particles, row_count, width), axis=1)

        lane = lax.broadcasted_iota(jnp.int32, (particles, message - width), 1)
        place = lax.broadcasted_iota(jnp.int32, (particles, message - width), 0)
        named = (lane // own_classes ^ lax.axis_index("cls")) * own_classes + lane % own_classes
        named = jnp.where(lane < classes, named, -1)
        meta = jnp.zeros(lane.shape, F32)
        assignments = assignments_ref[...]
        for j in range(assignments.shape[1]):
            meta = jnp.where(assignments[:, j : j + 1] == named, 1.0, meta)
        square = (particles, particles)
        same = lax.broadcasted_iota(jnp.int32, square, 0) == lax.broadcasted_iota(
            jnp.int32, square, 1
        )
        sharp = jnp.broadcast_to(sharp_ref[...].astype(F32), square)
        sharp = jnp.sum(jnp.where(same, sharp, 0.0), axis=1, keepdims=True)
        meta = jnp.where(lane == classes, sharp, meta)
        for n in range(particles):
            meta = jnp.where(
                (place == n) & (lane == classes + 1), best_ref[n].astype(F32), meta
            )
        out_ref[...] = jnp.concatenate([coeffs.astype(BF16), meta.astype(BF16)], axis=1)


def filter_images(
    images,
    group_ids,
    row_filters,
    column_filters,
    basis_rows,
    basis_columns,
    sharpness,
    best_rotation,
    assignments,
    own_classes,
    classes,
):
    particles, pixels = images.shape[:2]
    groups = row_filters.shape[0]
    row_count, column_count = basis_rows.shape[1], basis_columns.shape[1]
    message = row_count * column_count + classes + 2
    message += -message % LANES
    batch = 8 if particles % 8 == 0 else 1
    mask = jnp.asarray(soft_edge(pixels))
    whole2 = lambda s, *_: (0, 0)
    whole3 = lambda s, *_: (0, 0, 0)
    return pl.pallas_call(
        lambda *refs: filter_kernel(batch, own_classes, classes, *refs),
        out_shape=pltpu.VMEM((particles, message), BF16),
        grid_spec=pltpu.PrefetchScalarGridSpec(
            num_scalar_prefetch=2,
            grid=(particles // batch,),
            in_specs=[
                pl.BlockSpec((batch, pixels, pixels), lambda s, *_: (s, 0, 0)),
                pl.BlockSpec((groups, pixels, pixels), whole3),
                pl.BlockSpec((groups, pixels, pixels), whole3),
                pl.BlockSpec((pixels, pixels), whole2),
                pl.BlockSpec((row_count, pixels), whole2),
                pl.BlockSpec((column_count, pixels), whole2),
                pl.BlockSpec(assignments.shape, whole2),
                pl.BlockSpec((1, particles), whole2),
            ],
            out_specs=pl.BlockSpec((particles, message), whole2),
            scratch_shapes=[pltpu.VMEM((particles * row_count, pixels), F32)],
        ),
        compiler_params=pltpu.CompilerParams(
            dimension_semantics=("arbitrary",), vmem_limit_bytes=60 * 1024 * 1024
        ),
        cost_estimate=pl.CostEstimate(
            flops=4 * particles * pixels**3,
            bytes_accessed=2 * pixels * pixels * (particles + 2 * groups),
            transcendentals=0,
        ),
        name="filter_images",
    )(
        group_ids,
        best_rotation,
        images,
        row_filters,
        column_filters,
        mask,
        basis_rows.T,
        basis_columns.T,
        assignments,
        sharpness.reshape(1, particles),
    )


def cross(array, distance):
    sections, owners = lax.axis_size("section"), lax.axis_size("cls")
    pairs = [
        (s * owners + c, (s ^ 1) * owners + (c ^ distance))
        for s in range(sections)
        for c in range(owners)
    ]
    return lax.ppermute(array, ("section", "cls"), pairs)


def swap(array, axis, distance):
    size = lax.axis_size(axis)
    return lax.ppermute(array, axis, [(i, i ^ distance) for i in range(size)])


def log_add(a, b):
    top = jnp.maximum(a, b)
    return top + jnp.log(jnp.exp(a - top) + jnp.exp(b - top))


def iotas(shape):
    return lax.broadcasted_iota(jnp.int32, shape, 0), lax.broadcasted_iota(jnp.int32, shape, 1)


def one_hot(condition):
    return condition.astype(F32).astype(BF16)


def over_lanes(a, b):
    return lax.dot_general(a, b, (((1,), (1,)), ((), ())), preferred_element_type=F32)


def split_lanes(values, lanes):
    count = values.shape[1]
    high = values.astype(BF16)
    rest = values - high.astype(F32)
    middle = rest.astype(BF16)
    low = (rest - middle.astype(F32)).astype(BF16)
    k, lane = iotas((count, lanes))
    spread = jnp.dot(high, one_hot(lane == k), preferred_element_type=F32)
    spread = spread + jnp.dot(middle, one_hot(lane == k + count), preferred_element_type=F32)
    spread = spread + jnp.dot(low, one_hot(lane == k + 2 * count), preferred_element_type=F32)
    return spread.astype(BF16)


def join_lanes(parts, count, block, distance):
    k, n = iotas((parts.shape[1], count))
    source = (n // block ^ distance) * block + n % block
    here = (k == source) | (k == source + count) | (k == source + 2 * count)
    return jnp.dot(parts, one_hot(here), preferred_element_type=F32)


def score_kernel(
    particles, sections, classes, mine_ref, theirs_ref, own_ref, sibling_ref, out_ref, listed_ref
):
    local_rotations, width, _ = own_ref.shape
    section = lax.axis_index("section")
    held = sections * particles
    half = sections // 2
    rows = mine_ref.shape[0] // half
    spare = rows - particles
    fetched = classes // sections

    coeffs, meta, stack = [], [], []
    for m in range(sections):
        source = mine_ref if m < half else theirs_ref
        base = (m if m < half else sections - 1 - m) * rows
        coeffs.append(source[base : base + particles, :width])
        meta.append(source[base : base + particles, width:])
        stack.append(source[base + particles : base + rows, :width])
    coeffs = jnp.concatenate(coeffs, axis=0)
    meta = jnp.concatenate(meta, axis=0)
    stack = jnp.concatenate(stack, axis=0)

    q, k = iotas((classes, sections * spare))
    place = (k // spare ^ section) * fetched + k % spare
    refs = jnp.dot(
        one_hot((q == place) & (k % spare < fetched)), stack, preferred_element_type=F32
    ).astype(BF16)

    q, k = iotas((classes + 16, meta.shape[1]))
    turned_meta = over_lanes(one_hot(q == k), meta)
    listed_ref[...] = turned_meta[:classes]
    sharp = turned_meta[classes : classes + 1]
    best = meta[:, classes + 1 : classes + 2].astype(F32)

    turned_refs = jnp.concatenate(
        [
            jnp.dot(refs, rotations_ref[r], preferred_element_type=F32).astype(BF16)
            for rotations_ref in (own_ref, sibling_ref)
            for r in range(local_rotations)
        ],
        axis=0,
    )
    scores = over_lanes(turned_refs, coeffs) * sharp
    scores = scores.reshape(2 * local_rotations, classes, held)
    top = jnp.max(scores, axis=0)
    marg = top + jnp.log(jnp.sum(jnp.exp(scores - top[None]), axis=0))
    out_ref[held:, :] = split_lanes(marg, width)

    wide = coeffs.astype(F32)
    aligned = jnp.zeros((held, width), F32)
    for owner, rotations_ref in ((section, own_ref), (section ^ 1, sibling_ref)):
        offset = best - (owner * local_rotations).astype(F32)
        for r in range(local_rotations):
            chosen = jnp.where(offset == r, wide, 0.0).astype(BF16)
            aligned = aligned + over_lanes(chosen, rotations_ref[r])
    out_ref[:held, :] = aligned.astype(BF16)


def merge(particles, distance, held, mine_ref, theirs_ref):
    slots = held // particles
    theirs = [
        theirs_ref[(m ^ distance) * particles : (m ^ distance) * particles + particles, :]
        for m in range(slots)
    ]
    aligned = mine_ref[:held, :].astype(F32) + jnp.concatenate(theirs, axis=0).astype(F32)
    marg = log_add(
        join_lanes(mine_ref[held:, :], held, particles, 0),
        join_lanes(theirs_ref[held:, :], held, particles, distance),
    )
    return aligned.astype(BF16), marg


def sums_kernel(particles, distance, held, mine_ref, theirs_ref, listed_ref, out_ref, evidence_ref):
    aligned, marg = merge(particles, distance, held, mine_ref, theirs_ref)
    width = aligned.shape[1]
    top = jnp.max(marg, axis=0, keepdims=True)
    raised = jnp.exp(marg - top)
    evidence_ref[...] = top + jnp.log(jnp.sum(raised, axis=0, keepdims=True))
    picked = jnp.where(listed_ref[...] > 0.0, marg, -jnp.inf)
    raised = jnp.exp(picked - jnp.max(picked, axis=0, keepdims=True))
    weights = raised / jnp.sum(raised, axis=0, keepdims=True)
    weights = weights.astype(BF16)
    out_ref[:, :width] = jnp.dot(weights, aligned, preferred_element_type=F32)
    class_weights = jnp.sum(weights.astype(F32), axis=1, keepdims=True)
    out_ref[:, width:] = jnp.broadcast_to(class_weights, (marg.shape[0], LANES))


def small_call(kernel, name, *operands, out_shape, flops=0):
    read = sum(x.size * x.dtype.itemsize for x in operands)
    return pl.pallas_call(
        kernel,
        out_shape=out_shape,
        in_specs=[pl.BlockSpec(memory_space=pltpu.VMEM)] * len(operands),
        out_specs=jax.tree.map(lambda _: pl.BlockSpec(memory_space=pltpu.VMEM), out_shape),
        compiler_params=pltpu.CompilerParams(vmem_limit_bytes=16 * 1024 * 1024),
        cost_estimate=pl.CostEstimate(flops=flops, bytes_accessed=read, transcendentals=0),
        name=name,
    )(*operands)


def body(
    images,
    group_ids,
    row_filters,
    column_filters,
    basis_rows,
    basis_columns,
    rotations,
    references,
    sharpness,
    best_rotation,
    assignments,
):
    particles = images.shape[0]
    sections = lax.axis_size("section")
    owners = lax.axis_size("cls")
    own_classes, width = references.shape
    classes = own_classes * owners
    held = sections * particles

    sibling_rotations = swap(rotations, "section", 1)

    part = owners // sections
    refs = []
    for j in range(min(part, 2)):
        pairs = [
            (s * owners + c, s * owners + (c ^ (s * part + j or 1)))
            for s in range(sections)
            for c in range(owners)
        ]
        block = lax.ppermute(references, ("section", "cls"), pairs)
        if j == 0:
            block = jnp.where(lax.axis_index("section") == 0, references, block)
        refs.append(block)
    refs = jnp.concatenate(refs, axis=0)
    distance = 2
    while distance < part:
        refs = jnp.concatenate([refs, swap(refs, "cls", distance)], axis=0)
        distance *= 2

    message = filter_images(
        images,
        group_ids,
        row_filters,
        column_filters,
        basis_rows,
        basis_columns,
        sharpness,
        best_rotation,
        assignments,
        own_classes,
        classes,
    )
    refs = jnp.pad(refs, ((0, -refs.shape[0] % 16), (0, message.shape[1] - width)))
    message = jnp.concatenate([message, refs], axis=0)
    message = jnp.concatenate([message, swap(message, "section", 1)], axis=0)
    marg, listed = small_call(
        lambda *r: score_kernel(particles, sections, classes, *r),
        "scores",
        message,
        swap(message, "section", sections - 1),
        rotations,
        sibling_rotations,
        out_shape=(
            jax.ShapeDtypeStruct((held + classes, width), BF16),
            jax.ShapeDtypeStruct((classes, held), F32),
        ),
    )

    sums, evidence = small_call(
        lambda *r: sums_kernel(particles, sections - 1, held, *r),
        "class_sums",
        marg,
        swap(marg, "section", sections - 1),
        listed,
        out_shape=(
            jax.ShapeDtypeStruct((classes, width + LANES), F32),
            jax.ShapeDtypeStruct((1, held), F32),
        ),
    )

    distance = owners // 2
    while distance:
        half = distance * own_classes
        sums = sums[:half] + cross(sums[half:], distance)
        distance //= 2
    new_references = (sums[:, :width] + references.astype(F32)) / (sums[:, width : width + 1] + 1.0)
    return new_references, evidence[0, :particles]


def solution(mesh):
    in_specs = (
        P(("section", "cls"), None, None),
        P(("section", "cls")),
        P(),
        P(),
        P(),
        P(),
        P("section", None, None),
        P("cls", None),
        P(("section", "cls")),
        P(("section", "cls")),
        P(("section", "cls"), None),
    )
    out_specs = (P("cls", None), P(("section", "cls")))
    return jax.shard_map(body, mesh=mesh, in_specs=in_specs, out_specs=out_specs, check_vma=False)
```

time: 120 us -> 32.7 us (0.27)
  blocking collectives: 45.8 us -> 0 us
  local copies, waits for them, and re-layouts: 15.3 us -> 0.54 us
  between operations: 15 us -> 0.71 us
  matrix products: 10.9 us -> 0 us
  Pallas kernels: 0 us -> 6.54 us
  other arithmetic: 6.83 us -> 0.82 us
  waiting for transfers between devices: 13.5 us -> 10.3 us
  starting transfers between devices: 12 us -> 13.6 us
    all_gather x2 -> x0, blocking collectives: 27 us -> none  [the longest x1 20.8 us: body(): all_refs = lax.all_gather(references, 'cls', axis=0, tiled=True)]
    ppermute x0 -> x9, starting transfers between devices: none -> 13.6 us  [the longest x4 6.76 us: swap(): return lax.ppermute(array, axis, [(i, i ^ distance) for i in range(size)])]
    unnamed x2 -> x0, blocking collectives: 12.9 us -> none
    all_to_all x3 -> x0, starting transfers between devices: 12 us -> none  [the longest x1 5.52 us: body(): lax.all_to_all(buffer, 'cls', split_axis=0, concat_axis=0, tiled=True)]
    dot_general x6 -> x0, matrix products: 10.9 us -> none  [the longest x1 5.67 us: filter_images(): jnp.einsum('bij,bjk->bik', row_each, filtered_half, preferred_element_typ...]
    ppermute x0 -> x9, waiting for transfers between devices: none -> 10.3 us  [the longest x3 5.53 us: cross(): return lax.ppermute(array, ('section', 'cls'), pairs)]
    all_to_all x3 -> x0, waiting for transfers between devices: 6.73 us -> none  [the longest x1 6.72 us: body(): lax.all_to_all(buffer, 'cls', split_axis=0, concat_axis=0, tiled=True)]
    reduce_scatter x1 -> x0, waiting for transfers between devices: 6.72 us -> none  [body(): lax.psum_scatter(partial_rows.astype(jnp.bfloat16), 'section', scatter_di...]
  transfers between devices with their start and end apart: 4 -> 9, of which waited for: 2 -> 6; matrix products, arithmetic and copies ran while one was open for 10% -> 2% of each run, Pallas kernels for 0% -> 14%
where the time goes in v1:
time: 32.7 us; the launch traced here: 32.5 us
  starting transfers between devices  13.6 us (42%)
  waiting for transfers between devices  10.3 us (31%)
  Pallas kernels  6.54 us (20%)
  other arithmetic  0.82 us (3%)
  between operations  0.71 us (2%)
  local copies, waits for them, and re-layouts  0.54 us (2%)
    ppermute x4, starting transfers between devices, swap(): return lax.ppermute(array, axis, [(i, i ^ distance) for i in range(size)])  6.76 us
    ppermute x3, waiting for transfers between devices, cross(): return lax.ppermute(array, ('section', 'cls'), pairs)  5.53 us
    ppermute x4, waiting for transfers between devices, swap(): return lax.ppermute(array, axis, [(i, i ^ distance) for i in range(size)])  4.76 us
    pallas_call x1, Pallas kernels, filter_images(): pl.pallas_call(lambda *refs: filter_kernel(batch, own_classes, classes, *...  4.67 us
    ppermute x3, starting transfers between devices, cross(): return lax.ppermute(array, ('section', 'cls'), pairs)  4.19 us
    ppermute x2, starting transfers between devices, body(): block = lax.ppermute(references, ('section', 'cls'), pairs)  2.67 us
    pallas_call x2, Pallas kernels, small_call(): pl.pallas_call(kernel, out_shape=out_shape, in_specs=[pl.BlockSpec(memory...  1.88 us
    div x1, other arithmetic, body(): (sums[:, :width] + references.astype(F32)) / (sums[:, width:width + 1] +...  0.66 us
  transfers between devices with their start and end apart: 9, of which 6 were waited for; matrix products, arithmetic and copies ran while one was open for 2% of the time, Pallas kernels for 14%

profile of v1, /device:TPU:0, one launch (start us, length us, event | category | flops | bytes accessed | tf_op | source)
XLA Modules:
  0.0 32.5 jit_solution(8369623122324515788)
XLA Ops:
  0.6 0.5 %collective-permute-start.4 = (bf16[9,256,256]{2,1,0:T(8,128)(2,1)}, bf16[9,256,256]{2,1,0:T(8,128)(2,1)S(1)}, u32[]{:S(2)}, u32[]{:S(2)}) collective-permute-start(bf16[9,256,256]{2,1,0:T(8,128)(2,1)} %r_2_.1), channel_id=1, source_target_pairs={{0,8},{8,0},{16,24},{24,16},{1,9},{9,1},{17,25},{25,17},{2,10},{10... | collective-permute-start | bytes 3538952 | tf_op jit(solution)/shard_map/ppermute | solution.py:182
  1.2 2.6 %collective-permute-start = (bf16[2,256]{1,0:T(2,128)(2,1)}, bf16[2,256]{1,0:T(2,128)(2,1)S(1)}, u32[]{:S(2)}, u32[]{:S(2)}) collective-permute-start(bf16[2,256]{1,0:T(2,128)(2,1)} %param.19), channel_id=1, source_target_pairs={{0,1},{1,0},{2,3},{3,2},{4,5},{5,4},{6,7},{7,6},{8,10},{9,11},{10,... | collective-permute-start | bytes 3080 | tf_op jit(solution)/shard_map/ppermute | solution.py:352
  3.7 0.1 collective-permute-start.1
  3.8 4.7 %filter_images.1 = bf16[16,384]{1,0:T(8,128)(2,1)S(1)} custom-call(s32[16]{0:T(128)} %refs_0_.1, s32[16]{0:T(128)} %refs_1_.1, bf16[16,256,256]{2,1,0:T(8,128)(2,1)} %refs_2_.1, bf16[4,256,256]{2,1,0:T(8,128)(2,1)} %refs_3_.1, bf16[4,256,256]{2,1,0:T(8,128)(2,1)} %refs_4_.1, f32[256,256]{1,0:T(8,128)} %constant.13.clone.refs_5_, bf16[16,256]{1,0:T(8,128)(2,1)} %bitcast.5, ...), custom_call_target="tpu_custom_call" | custom-call | flops 1073741824 | bytes 3145728 | tf_op jit(solution)/shard_map/filter_images/pallas_call | solution.py:128
  8.5 0.0 collective-permute-done
  8.5 0.0 collective-permute-done.1
  8.6 1.3 %collective-permute-start.2 = (bf16[32,384]{1,0:T(8,128)(2,1)S(1)}, bf16[32,384]{1,0:T(8,128)(2,1)S(1)}, u32[]{:S(2)}, u32[]{:S(2)}) collective-permute-start(bf16[32,384]{1,0:T(8,128)(2,1)S(1)} %pad_maximum_fusion.1), channel_id=1, source_target_pairs={{0,8},{8,0},{16,24},{24,16},{1,9},{9,1},{17,25},{25,17},{2,10},{10... | collective-permute-start | bytes 73736 | tf_op jit(solution)/shard_map/ppermute | solution.py:182
  9.9 0.8 %collective-permute-done.2 = bf16[32,384]{1,0:T(8,128)(2,1)S(1)} collective-permute-done((bf16[32,384]{1,0:T(8,128)(2,1)S(1)}, bf16[32,384]{1,0:T(8,128)(2,1)S(1)}, u32[]{:S(2)}, u32[]{:S(2)}) %collective-permute-start.2) | collective-permute-done | bytes 24608 | tf_op jit(solution)/shard_map/ppermute | solution.py:182
  10.8 3.3 %collective-permute-start.3 = (bf16[64,384]{1,0:T(8,128)(2,1)S(1)}, bf16[64,384]{1,0:T(8,128)(2,1)S(1)}, u32[]{:S(2)}, u32[]{:S(2)}) collective-permute-start(bf16[64,384]{1,0:T(8,128)(2,1)S(1)} %pad_maximum_fusion.r_0_), channel_id=1, source_target_pairs={{0,24},{8,16},{16,8},{24,0},{1,25},{9,17},{17,9},{25,1},{2,26},{10... | collective-permute-start | bytes 147464 | tf_op jit(solution)/shard_map/ppermute | solution.py:182
  14.1 2.0 %collective-permute-done.3.r_1_ = bf16[64,384]{1,0:T(8,128)(2,1)S(1)} collective-permute-done((bf16[64,384]{1,0:T(8,128)(2,1)S(1)}, bf16[64,384]{1,0:T(8,128)(2,1)S(1)}, u32[]{:S(2)}, u32[]{:S(2)}) %collective-permute-start.3) | collective-permute-done | bytes 49184 | tf_op jit(solution)/shard_map/ppermute | solution.py:182
  16.0 0.0 collective-permute-done.4.r_3_
  16.0 1.5 %scores.1 = (bf16[80,256]{1,0:T(8,128)(2,1)S(1)}, f32[16,64]{1,0:T(8,128)S(1)}) custom-call(bf16[64,384]{1,0:T(8,128)(2,1)S(1)} %pad_maximum_fusion.r_0_, bf16[64,384]{1,0:T(8,128)(2,1)S(1)} %collective-permute-done.3.r_1_, bf16[9,256,256]{2,1,0:T(8,128)(2,1)S(1)} %copy-done, bf16[9,256,256]{2,1,0:T(8,128)(2,1)S(1)} %collective-permute-done.4.r_3_), custom_call_target="tpu_custom_call" | custom-call | bytes 2457600 | tf_op jit(solution)/shard_map/scores/pallas_call | solution.py:311
  17.5 1.6 %collective-permute-start.5 = (bf16[80,256]{1,0:T(8,128)(2,1)S(1)}, bf16[80,256]{1,0:T(8,128)(2,1)S(1)}, u32[]{:S(2)}, u32[]{:S(2)}) collective-permute-start(bf16[80,256]{1,0:T(8,128)(2,1)S(1)} %get-tuple-element.6.r_0_), channel_id=1, source_target_pairs={{0,24},{8,16},{16,8},{24,0},{1,25},{9,17},{17,9},{25,1},{2,26},{10... | collective-permute-start | bytes 122888 | tf_op jit(solution)/shard_map/ppermute | solution.py:182
  19.1 2.0 %collective-permute-done.5.r_1_ = bf16[80,256]{1,0:T(8,128)(2,1)S(1)} collective-permute-done((bf16[80,256]{1,0:T(8,128)(2,1)S(1)}, bf16[80,256]{1,0:T(8,128)(2,1)S(1)}, u32[]{:S(2)}, u32[]{:S(2)}) %collective-permute-start.5) | collective-permute-done | bytes 40992 | tf_op jit(solution)/shard_map/ppermute | solution.py:182
  21.1 0.4 %class_sums.1 = (f32[16,384]{1,0:T(8,128)S(1)}, f32[1,64]{1,0:T(1,128)S(1)}) custom-call(bf16[80,256]{1,0:T(8,128)(2,1)S(1)} %get-tuple-element.6.r_0_, bf16[80,256]{1,0:T(8,128)(2,1)S(1)} %collective-permute-done.5.r_1_, f32[16,64]{1,0:T(8,128)S(1)} %get-tuple-element.7.r_2_), custom_call_target="tpu_custom_call" | custom-call | bytes 86016 | tf_op jit(solution)/shard_map/class_sums/pallas_call | solution.py:311
  21.5 1.8 %collective-permute-start.6 = (f32[8,384]{1,0:T(8,128)S(1)}, f32[8,384]{1,0:T(8,128)S(1)}, u32[]{:S(2)}, u32[]{:S(2)}) collective-permute-start(f32[8,384]{1,0:T(8,128)S(1)} %slice.28), channel_id=1, source_target_pairs={{0,12},{1,13},{2,14},{3,15},{4,8},{5,9},{6,10},{7,11},{8,4},{9,5},... | collective-permute-start | bytes 36872 | tf_op jit(solution)/shard_map/ppermute | solution.py:177
  23.3 2.2 %collective-permute-done.6 = f32[8,384]{1,0:T(8,128)S(1)} collective-permute-done((f32[8,384]{1,0:T(8,128)S(1)}, f32[8,384]{1,0:T(8,128)S(1)}, u32[]{:S(2)}, u32[]{:S(2)}) %collective-permute-start.6) | collective-permute-done | bytes 12320 | tf_op jit(solution)/shard_map/ppermute | solution.py:177
  25.5 1.3 %collective-permute-start.7 = (f32[4,384]{1,0:T(4,128)S(1)}, f32[4,384]{1,0:T(4,128)S(1)}, u32[]{:S(2)}, u32[]{:S(2)}) collective-permute-start(f32[4,384]{1,0:T(4,128)S(1)} %slice.37), channel_id=1, source_target_pairs={{0,10},{1,11},{2,8},{3,9},{4,14},{5,15},{6,12},{7,13},{8,2},{9,3},... | collective-permute-start | bytes 18440 | tf_op jit(solution)/shard_map/ppermute | solution.py:177
  26.9 1.8 %collective-permute-done.7 = f32[4,384]{1,0:T(4,128)S(1)} collective-permute-done((f32[4,384]{1,0:T(4,128)S(1)}, f32[4,384]{1,0:T(4,128)S(1)}, u32[]{:S(2)}, u32[]{:S(2)}) %collective-permute-start.7) | collective-permute-done | bytes 6176 | tf_op jit(solution)/shard_map/ppermute | solution.py:177
  28.7 1.0 %collective-permute-start.8 = (f32[2,384]{1,0:T(2,128)S(1)}, f32[2,384]{1,0:T(2,128)S(1)}, u32[]{:S(2)}, u32[]{:S(2)}) collective-permute-start(f32[2,384]{1,0:T(2,128)S(1)} %slice.39), channel_id=1, source_target_pairs={{0,9},{1,8},{2,11},{3,10},{4,13},{5,12},{6,15},{7,14},{8,1},{9,0},... | collective-permute-start | bytes 9224 | tf_op jit(solution)/shard_map/ppermute | solution.py:177
  29.7 0.5 %slice_bitcast_fusion = f32[16]{0:T(128)} fusion(f32[1,64]{1,0:T(1,128)S(1)} %get-tuple-element.9), kind=kLoop, calls=%fused_computation.18 | loop fusion | bytes 128 | tf_op jit(solution)/shard_map/squeeze | solution.py:409
  30.2 1.5 %collective-permute-done.8 = f32[2,384]{1,0:T(2,128)S(1)} collective-permute-done((f32[2,384]{1,0:T(2,128)S(1)}, f32[2,384]{1,0:T(2,128)S(1)}, u32[]{:S(2)}, u32[]{:S(2)}) %collective-permute-start.8) | collective-permute-done | bytes 3104 | tf_op jit(solution)/shard_map/ppermute | solution.py:177
  31.8 0.1 fusion.7
  31.9 0.7 %fusion.6 = f32[2,256]{1,0:T(2,128)} fusion(f32[2,384]{1,0:T(2,128)S(1)} %slice_add_fusion.2, bf16[2,256]{1,0:T(2,128)(2,1)S(1)} %copy-done.1, f32[2]{0:T(128)S(1)} %fusion.7), kind=kLoop, calls=%fused_computation.14 | loop fusion | flops 1536 | bytes 5128 | tf_op jit(solution)/shard_map/div | solution.py:408
  (14 shorter events, 0.1 us)
Async XLA Ops:
  0.6 15.4 %collective-permute-start.4 = (bf16[9,256,256]{2,1,0:T(8,128)(2,1)}, bf16[9,256,256]{2,1,0:T(8,128)(2,1)S(1)}, u32[]{:S(2)}, u32[]{:S(2)}) collective-permute-start(bf16[9,256,256]{2,1,0:T(8,128)(2,1)} %r_2_.1), channel_id=1, source_target_pairs={{0,8},{8,0},{16,24},{24,16},{1,9},{9,1},{17,25},{25,17},{2,10},{10... | collective-permute-start | bytes 3538952 | tf_op jit(solution)/shard_map/ppermute | solution.py:182
  1.2 7.4 %collective-permute-start = (bf16[2,256]{1,0:T(2,128)(2,1)}, bf16[2,256]{1,0:T(2,128)(2,1)S(1)}, u32[]{:S(2)}, u32[]{:S(2)}) collective-permute-start(bf16[2,256]{1,0:T(2,128)(2,1)} %param.19), channel_id=1, source_target_pairs={{0,1},{1,0},{2,3},{3,2},{4,5},{5,4},{6,7},{7,6},{8,10},{9,11},{10,... | collective-permute-start | bytes 3080 | tf_op jit(solution)/shard_map/ppermute | solution.py:352
  3.7 4.8 %collective-permute-start.1 = (bf16[2,256]{1,0:T(2,128)(2,1)}, bf16[2,256]{1,0:T(2,128)(2,1)S(1)}, u32[]{:S(2)}, u32[]{:S(2)}) collective-permute-start(bf16[2,256]{1,0:T(2,128)(2,1)} %param.19), channel_id=1, source_target_pairs={{0,1},{1,0},{2,3},{3,2},{4,5},{5,4},{6,7},{7,6},{8,11},{9,10},{10,... | collective-permute-start | bytes 3080 | tf_op jit(solution)/shard_map/ppermute | solution.py:352
  3.8 4.7 %copy-start.1 = (bf16[2,256]{1,0:T(2,128)(2,1)S(1)}, bf16[2,256]{1,0:T(2,128)(2,1)}, u32[]{:S(2)}) copy-start(bf16[2,256]{1,0:T(2,128)(2,1)} %param.19) | copy-start | bytes 3076
  3.8 12.2 %copy-start = (bf16[9,256,256]{2,1,0:T(8,128)(2,1)S(1)}, bf16[9,256,256]{2,1,0:T(8,128)(2,1)}, u32[]{:S(2)}) copy-start(bf16[9,256,256]{2,1,0:T(8,128)(2,1)} %r_2_.1) | copy-start | bytes 3538948
  8.6 2.2 %collective-permute-start.2 = (bf16[32,384]{1,0:T(8,128)(2,1)S(1)}, bf16[32,384]{1,0:T(8,128)(2,1)S(1)}, u32[]{:S(2)}, u32[]{:S(2)}) collective-permute-start(bf16[32,384]{1,0:T(8,128)(2,1)S(1)} %pad_maximum_fusion.1), channel_id=1, source_target_pairs={{0,8},{8,0},{16,24},{24,16},{1,9},{9,1},{17,25},{25,17},{2,10},{10... | collective-permute-start | bytes 73736 | tf_op jit(solution)/shard_map/ppermute | solution.py:182
  10.8 5.2 %collective-permute-start.3 = (bf16[64,384]{1,0:T(8,128)(2,1)S(1)}, bf16[64,384]{1,0:T(8,128)(2,1)S(1)}, u32[]{:S(2)}, u32[]{:S(2)}) collective-permute-start(bf16[64,384]{1,0:T(8,128)(2,1)S(1)} %pad_maximum_fusion.r_0_), channel_id=1, source_target_pairs={{0,24},{8,16},{16,8},{24,0},{1,25},{9,17},{17,9},{25,1},{2,26},{10... | collective-permute-start | bytes 147464 | tf_op jit(solution)/shard_map/ppermute | solution.py:182
  17.5 3.6 %collective-permute-start.5 = (bf16[80,256]{1,0:T(8,128)(2,1)S(1)}, bf16[80,256]{1,0:T(8,128)(2,1)S(1)}, u32[]{:S(2)}, u32[]{:S(2)}) collective-permute-start(bf16[80,256]{1,0:T(8,128)(2,1)S(1)} %get-tuple-element.6.r_0_), channel_id=1, source_target_pairs={{0,24},{8,16},{16,8},{24,0},{1,25},{9,17},{17,9},{25,1},{2,26},{10... | collective-permute-start | bytes 122888 | tf_op jit(solution)/shard_map/ppermute | solution.py:182
  21.5 4.0 %collective-permute-start.6 = (f32[8,384]{1,0:T(8,128)S(1)}, f32[8,384]{1,0:T(8,128)S(1)}, u32[]{:S(2)}, u32[]{:S(2)}) collective-permute-start(f32[8,384]{1,0:T(8,128)S(1)} %slice.28), channel_id=1, source_target_pairs={{0,12},{1,13},{2,14},{3,15},{4,8},{5,9},{6,10},{7,11},{8,4},{9,5},... | collective-permute-start | bytes 36872 | tf_op jit(solution)/shard_map/ppermute | solution.py:177
  25.5 3.1 %collective-permute-start.7 = (f32[4,384]{1,0:T(4,128)S(1)}, f32[4,384]{1,0:T(4,128)S(1)}, u32[]{:S(2)}, u32[]{:S(2)}) collective-permute-start(f32[4,384]{1,0:T(4,128)S(1)} %slice.37), channel_id=1, source_target_pairs={{0,10},{1,11},{2,8},{3,9},{4,14},{5,15},{6,12},{7,13},{8,2},{9,3},... | collective-permute-start | bytes 18440 | tf_op jit(solution)/shard_map/ppermute | solution.py:177
  28.7 3.1 %collective-permute-start.8 = (f32[2,384]{1,0:T(2,128)S(1)}, f32[2,384]{1,0:T(2,128)S(1)}, u32[]{:S(2)}, u32[]{:S(2)}) collective-permute-start(f32[2,384]{1,0:T(2,128)S(1)} %slice.39), channel_id=1, source_target_pairs={{0,9},{1,8},{2,11},{3,10},{4,13},{5,12},{6,15},{7,14},{8,1},{9,0},... | collective-permute-start | bytes 9224 | tf_op jit(solution)/shard_map/ppermute | solution.py:177

commit v2 on v1

--- a/solution.py
+++ b/solution.py
@@ -220,31 +220,25 @@
 
 
 def score_kernel(
-    particles, sections, classes, mine_ref, theirs_ref, own_ref, sibling_ref, out_ref, listed_ref
+    particles, sections, own_classes, classes, *refs
 ):
+    messages, (own_ref, sibling_ref, out_ref, listed_ref) = refs[:sections], refs[sections:]
     local_rotations, width, _ = own_ref.shape
     section = lax.axis_index("section")
     held = sections * particles
-    half = sections // 2
-    rows = mine_ref.shape[0] // half
-    spare = rows - particles
+    spare = messages[0].shape[0] - particles
+
+    coeffs = jnp.concatenate([ref[:particles, :width] for ref in messages], axis=0)
+    meta = jnp.concatenate([ref[:particles, width:] for ref in messages], axis=0)
+    stack = jnp.concatenate([ref[particles:, :width] for ref in messages], axis=0)
+
+    q, k = iotas((classes, sections * spare))
+    row = k % spare
+    place = (k // spare ^ section) + row // own_classes * sections
+    place = place * own_classes + row % own_classes
     fetched = classes // sections
-
-    coeffs, meta, stack = [], [], []
-    for m in range(sections):
-        source = mine_ref if m < half else theirs_ref
-        base = (m if m < half else sections - 1 - m) * rows
-        coeffs.append(source[base : base + particles, :width])
-        meta.append(source[base : base + particles, width:])
-        stack.append(source[base + particles : base + rows, :width])
-    coeffs = jnp.concatenate(coeffs, axis=0)
-    meta = jnp.concatenate(meta, axis=0)
-    stack = jnp.concatenate(stack, axis=0)
-
-    q, k = iotas((classes, sections * spare))
-    place = (k // spare ^ section) * fetched + k % spare
     refs = jnp.dot(
-        one_hot((q == place) & (k % spare < fetched)), stack, preferred_element_type=F32
+        one_hot((q == place) & (row < fetched)), stack, preferred_element_type=F32
     ).astype(BF16)
 
     q, k = iotas((classes + 16, meta.shape[1]))
@@ -341,21 +335,20 @@
 
     sibling_rotations = swap(rotations, "section", 1)
 
-    part = owners // sections
     refs = []
-    for j in range(min(part, 2)):
+    for first in range(0, min(owners, 2 * sections), sections):
         pairs = [
-            (s * owners + c, s * owners + (c ^ (s * part + j or 1)))
+            (s * owners + c, s * owners + (c ^ (first + s or 1)))
             for s in range(sections)
             for c in range(owners)
         ]
         block = lax.ppermute(references, ("section", "cls"), pairs)
-        if j == 0:
+        if first == 0:
             block = jnp.where(lax.axis_index("section") == 0, references, block)
         refs.append(block)
     refs = jnp.concatenate(refs, axis=0)
-    distance = 2
-    while distance < part:
+    distance = 2 * sections
+    while distance < owners:
         refs = jnp.concatenate([refs, swap(refs, "cls", distance)], axis=0)
         distance *= 2
 
@@ -374,12 +367,11 @@
     )
     refs = jnp.pad(refs, ((0, -refs.shape[0] % 16), (0, message.shape[1] - width)))
     message = jnp.concatenate([message, refs], axis=0)
-    message = jnp.concatenate([message, swap(message, "section", 1)], axis=0)
     marg, listed = small_call(
-        lambda *r: score_kernel(particles, sections, classes, *r),
+        lambda *r: score_kernel(particles, sections, own_classes, classes, *r),
         "scores",
         message,
-        swap(message, "section", sections - 1),
+        *[swap(message, "section", k) for k in range(1, sections)],
         rotations,
         sibling_rotations,
         out_shape=(
@@ -405,7 +397,8 @@
         half = distance * own_classes
         sums = sums[:half] + cross(sums[half:], distance)
         distance //= 2
-    new_references = (sums[:, :width] + references.astype(F32)) / (sums[:, width : width + 1] + 1.0)
+    class_weights = jnp.concatenate([sums[:, width:]] * (width // LANES), axis=1)
+    new_references = (sums[:, :width] + references.astype(F32)) / (class_weights + 1.0)
     return new_references, evidence[0, :particles]
 
 

time: 32.7 us -> 33.2 us (1.015)
  waiting for transfers between devices: 10.3 us -> 16.5 us
  starting transfers between devices: 13.6 us -> 8.15 us
    ppermute x4 -> x5, starting transfers between devices: 6.76 us -> 2.66 us  [swap(): return lax.ppermute(array, axis, [(i, i ^ distance) for i in range(size)])]
    ppermute x3, waiting for transfers between devices: 5.53 us -> 9.41 us  [cross(): return lax.ppermute(array, ('section', 'cls'), pairs)]
    ppermute x3, starting transfers between devices: 4.19 us -> 0.31 us  [cross(): return lax.ppermute(array, ('section', 'cls'), pairs)]
    ppermute x2, starting transfers between devices: 2.67 us -> 5.18 us  [body(): block = lax.ppermute(references, ('section', 'cls'), pairs)]
    ppermute x4 -> x5, waiting for transfers between devices: 4.76 us -> 7.05 us  [swap(): return lax.ppermute(array, axis, [(i, i ^ distance) for i in range(size)])]
  transfers between devices with their start and end apart: 9 -> 10, of which waited for: 6 -> 6; matrix products, arithmetic and copies ran while one was open for 2% -> 2% of each run, Pallas kernels for 14% -> 14%
where the time goes in v2:
time: 33.2 us; the launch traced here: 33.1 us
  waiting for transfers between devices  16.5 us (50%)
  starting transfers between devices  8.15 us (25%)
  Pallas kernels  6.55 us (20%)
  between operations  0.73 us (2%)
  other arithmetic  0.63 us (2%)
  local copies, waits for them, and re-layouts  0.54 us (2%)
    ppermute x3, waiting for transfers between devices, cross(): return lax.ppermute(array, ('section', 'cls'), pairs)  9.41 us
    ppermute x5, waiting for transfers between devices, swap(): return lax.ppermute(array, axis, [(i, i ^ distance) for i in range(size)])  7.05 us
    ppermute x2, starting transfers between devices, body(): block = lax.ppermute(references, ('section', 'cls'), pairs)  5.18 us
    pallas_call x1, Pallas kernels, filter_images(): pl.pallas_call(lambda *refs: filter_kernel(batch, own_classes, classes, *...  4.66 us
    ppermute x5, starting transfers between devices, swap(): return lax.ppermute(array, axis, [(i, i ^ distance) for i in range(size)])  2.66 us
    pallas_call x2, Pallas kernels, small_call(): pl.pallas_call(kernel, out_shape=out_shape, in_specs=[pl.BlockSpec(memory...  1.88 us
  transfers between devices with their start and end apart: 10, of which 6 were waited for; matrix products, arithmetic and copies ran while one was open for 2% of the time, Pallas kernels for 14%

profile of v2, /device:TPU:0, one launch (start us, length us, event | category | flops | bytes accessed | tf_op | source)
XLA Modules:
  0.0 33.1 jit_solution(4749147998729223563)
XLA Ops:
  0.6 0.5 %collective-permute-start.5 = (bf16[9,256,256]{2,1,0:T(8,128)(2,1)}, bf16[9,256,256]{2,1,0:T(8,128)(2,1)S(1)}, u32[]{:S(2)}, u32[]{:S(2)}) collective-permute-start(bf16[9,256,256]{2,1,0:T(8,128)(2,1)} %r_4_.1), channel_id=1, source_target_pairs={{0,8},{8,0},{16,24},{24,16},{1,9},{9,1},{17,25},{25,17},{2,10},{10... | collective-permute-start | bytes 3538952 | tf_op jit(solution)/shard_map/ppermute | solution.py:182
  1.2 2.6 %collective-permute-start = (bf16[2,256]{1,0:T(2,128)(2,1)}, bf16[2,256]{1,0:T(2,128)(2,1)S(1)}, u32[]{:S(2)}, u32[]{:S(2)}) collective-permute-start(bf16[2,256]{1,0:T(2,128)(2,1)} %param.19), channel_id=1, source_target_pairs={{0,1},{1,0},{2,3},{3,2},{4,5},{5,4},{6,7},{7,6},{8,9},{9,8},{10,11... | collective-permute-start | bytes 3080 | tf_op jit(solution)/shard_map/ppermute | solution.py:345
  3.7 2.6 %collective-permute-start.1 = (bf16[2,256]{1,0:T(2,128)(2,1)}, bf16[2,256]{1,0:T(2,128)(2,1)S(1)}, u32[]{:S(2)}, u32[]{:S(2)}) collective-permute-start(bf16[2,256]{1,0:T(2,128)(2,1)} %param.19), channel_id=1, source_target_pairs={{0,4},{1,5},{2,6},{3,7},{4,0},{5,1},{6,2},{7,3},{8,13},{9,12},{10,... | collective-permute-start | bytes 3080 | tf_op jit(solution)/shard_map/ppermute | solution.py:345
  6.3 4.7 %filter_images.1 = bf16[16,384]{1,0:T(8,128)(2,1)S(1)} custom-call(s32[16]{0:T(128)} %refs_0_.1, s32[16]{0:T(128)} %refs_1_.1, bf16[16,256,256]{2,1,0:T(8,128)(2,1)} %refs_2_.1, bf16[4,256,256]{2,1,0:T(8,128)(2,1)} %refs_3_.1, bf16[4,256,256]{2,1,0:T(8,128)(2,1)} %refs_4_.1, f32[256,256]{1,0:T(8,128)} %constant.13.clone.refs_5_, bf16[16,256]{1,0:T(8,128)(2,1)} %bitcast.5, ...), custom_call_target="tpu_custom_call" | custom-call | flops 1073741824 | bytes 3145728 | tf_op jit(solution)/shard_map/filter_images/pallas_call | solution.py:128
  11.1 0.0 collective-permute-done.1
  11.1 1.9 %collective-permute-start.4 = (bf16[32,384]{1,0:T(8,128)(2,1)S(1)}, bf16[32,384]{1,0:T(8,128)(2,1)S(1)}, u32[]{:S(2)}, u32[]{:S(2)}) collective-permute-start(bf16[32,384]{1,0:T(8,128)(2,1)S(1)} %pad_maximum_fusion.r_0_), channel_id=1, source_target_pairs={{0,24},{8,16},{16,8},{24,0},{1,25},{9,17},{17,9},{25,1},{2,26},{10... | collective-permute-start | bytes 73736 | tf_op jit(solution)/shard_map/ppermute | solution.py:182
  13.0 0.0 collective-permute-start.3
  13.0 0.2 collective-permute-start.2
  13.2 1.5 %collective-permute-done.4.r_3_ = bf16[32,384]{1,0:T(8,128)(2,1)S(1)} collective-permute-done((bf16[32,384]{1,0:T(8,128)(2,1)S(1)}, bf16[32,384]{1,0:T(8,128)(2,1)S(1)}, u32[]{:S(2)}, u32[]{:S(2)}) %collective-permute-start.4) | collective-permute-done | bytes 24608 | tf_op jit(solution)/shard_map/ppermute | solution.py:182
  14.7 2.1 %collective-permute-done.3.r_2_ = bf16[32,384]{1,0:T(8,128)(2,1)S(1)} collective-permute-done((bf16[32,384]{1,0:T(8,128)(2,1)S(1)}, bf16[32,384]{1,0:T(8,128)(2,1)S(1)}, u32[]{:S(2)}, u32[]{:S(2)}) %collective-permute-start.3) | collective-permute-done | bytes 24608 | tf_op jit(solution)/shard_map/ppermute | solution.py:182
  16.8 0.0 collective-permute-done.2.r_1_
  16.8 0.0 collective-permute-done.5.r_5_
  16.8 1.5 %scores.1 = (bf16[80,256]{1,0:T(8,128)(2,1)S(1)}, f32[16,64]{1,0:T(8,128)S(1)}) custom-call(bf16[32,384]{1,0:T(8,128)(2,1)S(1)} %pad_maximum_fusion.r_0_, bf16[32,384]{1,0:T(8,128)(2,1)S(1)} %collective-permute-done.2.r_1_, bf16[32,384]{1,0:T(8,128)(2,1)S(1)} %collective-permute-done.3.r_2_, bf16[32,384]{1,0:T(8,128)(2,1)S(1)} %collective-permute-done.4.r_3_, ...), custom_call_target="tpu_custom_call" | custom-call | bytes 2457600 | tf_op jit(solution)/shard_map/scores/pallas_call | solution.py:305
  18.3 0.1 collective-permute-start.6
  18.4 3.4 %collective-permute-done.6.r_1_ = bf16[80,256]{1,0:T(8,128)(2,1)S(1)} collective-permute-done((bf16[80,256]{1,0:T(8,128)(2,1)S(1)}, bf16[80,256]{1,0:T(8,128)(2,1)S(1)}, u32[]{:S(2)}, u32[]{:S(2)}) %collective-permute-start.6) | collective-permute-done | bytes 40992 | tf_op jit(solution)/shard_map/ppermute | solution.py:182
  21.8 0.4 %class_sums.1 = (f32[16,384]{1,0:T(8,128)S(1)}, f32[1,64]{1,0:T(1,128)S(1)}) custom-call(bf16[80,256]{1,0:T(8,128)(2,1)S(1)} %get-tuple-element.6.r_0_, bf16[80,256]{1,0:T(8,128)(2,1)S(1)} %collective-permute-done.6.r_1_, f32[16,64]{1,0:T(8,128)S(1)} %get-tuple-element.7.r_2_), custom_call_target="tpu_custom_call" | custom-call | bytes 86016 | tf_op jit(solution)/shard_map/class_sums/pallas_call | solution.py:305
  22.2 0.0 collective-permute-start.7
  22.2 4.0 %collective-permute-done.7 = f32[8,384]{1,0:T(8,128)S(1)} collective-permute-done((f32[8,384]{1,0:T(8,128)S(1)}, f32[8,384]{1,0:T(8,128)S(1)}, u32[]{:S(2)}, u32[]{:S(2)}) %collective-permute-start.7) | collective-permute-done | bytes 12320 | tf_op jit(solution)/shard_map/ppermute | solution.py:177
  26.3 0.1 collective-permute-start.8
  26.3 3.0 %collective-permute-done.8 = f32[4,384]{1,0:T(4,128)S(1)} collective-permute-done((f32[4,384]{1,0:T(4,128)S(1)}, f32[4,384]{1,0:T(4,128)S(1)}, u32[]{:S(2)}, u32[]{:S(2)}) %collective-permute-start.8) | collective-permute-done | bytes 6176 | tf_op jit(solution)/shard_map/ppermute | solution.py:177
  29.4 0.2 collective-permute-start.9
  29.6 0.5 %slice_bitcast_fusion = f32[16]{0:T(128)} fusion(f32[1,64]{1,0:T(1,128)S(1)} %get-tuple-element.9), kind=kLoop, calls=%fused_computation.16 | loop fusion | bytes 128 | tf_op jit(solution)/shard_map/squeeze | solution.py:402
  30.1 2.3 %collective-permute-done.9 = f32[2,384]{1,0:T(2,128)S(1)} collective-permute-done((f32[2,384]{1,0:T(2,128)S(1)}, f32[2,384]{1,0:T(2,128)S(1)}, u32[]{:S(2)}, u32[]{:S(2)}) %collective-permute-start.9) | collective-permute-done | bytes 3104 | tf_op jit(solution)/shard_map/ppermute | solution.py:177
  32.5 0.6 %fusion.6 = f32[2,256]{1,0:T(2,128)} fusion(f32[2,384]{1,0:T(2,128)S(1)} %slice_add_fusion.2, f32[2,128]{1,0:T(2,128)S(1)} %slice.41, bf16[2,256]{1,0:T(2,128)(2,1)S(1)} %copy-done.1), kind=kLoop, calls=%fused_computation.13 | loop fusion | flops 2560 | bytes 6144 | tf_op jit(solution)/shard_map/div | solution.py:401
  (15 shorter events, 0.1 us)
Async XLA Ops:
  0.6 16.2 %collective-permute-start.5 = (bf16[9,256,256]{2,1,0:T(8,128)(2,1)}, bf16[9,256,256]{2,1,0:T(8,128)(2,1)S(1)}, u32[]{:S(2)}, u32[]{:S(2)}) collective-permute-start(bf16[9,256,256]{2,1,0:T(8,128)(2,1)} %r_4_.1), channel_id=1, source_target_pairs={{0,8},{8,0},{16,24},{24,16},{1,9},{9,1},{17,25},{25,17},{2,10},{10... | collective-permute-start | bytes 3538952 | tf_op jit(solution)/shard_map/ppermute | solution.py:182
  1.2 9.9 %collective-permute-start = (bf16[2,256]{1,0:T(2,128)(2,1)}, bf16[2,256]{1,0:T(2,128)(2,1)S(1)}, u32[]{:S(2)}, u32[]{:S(2)}) collective-permute-start(bf16[2,256]{1,0:T(2,128)(2,1)} %param.19), channel_id=1, source_target_pairs={{0,1},{1,0},{2,3},{3,2},{4,5},{5,4},{6,7},{7,6},{8,9},{9,8},{10,11... | collective-permute-start | bytes 3080 | tf_op jit(solution)/shard_map/ppermute | solution.py:345
  3.7 7.3 %collective-permute-start.1 = (bf16[2,256]{1,0:T(2,128)(2,1)}, bf16[2,256]{1,0:T(2,128)(2,1)S(1)}, u32[]{:S(2)}, u32[]{:S(2)}) collective-permute-start(bf16[2,256]{1,0:T(2,128)(2,1)} %param.19), channel_id=1, source_target_pairs={{0,4},{1,5},{2,6},{3,7},{4,0},{5,1},{6,2},{7,3},{8,13},{9,12},{10,... | collective-permute-start | bytes 3080 | tf_op jit(solution)/shard_map/ppermute | solution.py:345
  6.3 4.7 %copy-start.1 = (bf16[2,256]{1,0:T(2,128)(2,1)S(1)}, bf16[2,256]{1,0:T(2,128)(2,1)}, u32[]{:S(2)}) copy-start(bf16[2,256]{1,0:T(2,128)(2,1)} %param.19) | copy-start | bytes 3076
  6.3 10.5 %copy-start = (bf16[9,256,256]{2,1,0:T(8,128)(2,1)S(1)}, bf16[9,256,256]{2,1,0:T(8,128)(2,1)}, u32[]{:S(2)}) copy-start(bf16[9,256,256]{2,1,0:T(8,128)(2,1)} %r_4_.1) | copy-start | bytes 3538948
  11.1 3.6 %collective-permute-start.4 = (bf16[32,384]{1,0:T(8,128)(2,1)S(1)}, bf16[32,384]{1,0:T(8,128)(2,1)S(1)}, u32[]{:S(2)}, u32[]{:S(2)}) collective-permute-start(bf16[32,384]{1,0:T(8,128)(2,1)S(1)} %pad_maximum_fusion.r_0_), channel_id=1, source_target_pairs={{0,24},{8,16},{16,8},{24,0},{1,25},{9,17},{17,9},{25,1},{2,26},{10... | collective-permute-start | bytes 73736 | tf_op jit(solution)/shard_map/ppermute | solution.py:182
  13.0 3.8 %collective-permute-start.3 = (bf16[32,384]{1,0:T(8,128)(2,1)S(1)}, bf16[32,384]{1,0:T(8,128)(2,1)S(1)}, u32[]{:S(2)}, u32[]{:S(2)}) collective-permute-start(bf16[32,384]{1,0:T(8,128)(2,1)S(1)} %pad_maximum_fusion.r_0_), channel_id=1, source_target_pairs={{0,16},{8,24},{16,0},{24,8},{1,17},{9,25},{17,1},{25,9},{2,18},{10... | collective-permute-start | bytes 73736 | tf_op jit(solution)/shard_map/ppermute | solution.py:182
  13.0 3.8 %collective-permute-start.2 = (bf16[32,384]{1,0:T(8,128)(2,1)S(1)}, bf16[32,384]{1,0:T(8,128)(2,1)S(1)}, u32[]{:S(2)}, u32[]{:S(2)}) collective-permute-start(bf16[32,384]{1,0:T(8,128)(2,1)S(1)} %pad_maximum_fusion.r_0_), channel_id=1, source_target_pairs={{0,8},{8,0},{16,24},{24,16},{1,9},{9,1},{17,25},{25,17},{2,10},{10... | collective-permute-start | bytes 73736 | tf_op jit(solution)/shard_map/ppermute | solution.py:182
  18.3 3.5 %collective-permute-start.6 = (bf16[80,256]{1,0:T(8,128)(2,1)S(1)}, bf16[80,256]{1,0:T(8,128)(2,1)S(1)}, u32[]{:S(2)}, u32[]{:S(2)}) collective-permute-start(bf16[80,256]{1,0:T(8,128)(2,1)S(1)} %get-tuple-element.6.r_0_), channel_id=1, source_target_pairs={{0,24},{8,16},{16,8},{24,0},{1,25},{9,17},{17,9},{25,1},{2,26},{10... | collective-permute-start | bytes 122888 | tf_op jit(solution)/shard_map/ppermute | solution.py:182
  22.2 4.0 %collective-permute-start.7 = (f32[8,384]{1,0:T(8,128)S(1)}, f32[8,384]{1,0:T(8,128)S(1)}, u32[]{:S(2)}, u32[]{:S(2)}) collective-permute-start(f32[8,384]{1,0:T(8,128)S(1)} %slice.28), channel_id=1, source_target_pairs={{0,12},{1,13},{2,14},{3,15},{4,8},{5,9},{6,10},{7,11},{8,4},{9,5},... | collective-permute-start | bytes 36872 | tf_op jit(solution)/shard_map/ppermute | solution.py:177
  26.3 3.1 %collective-permute-start.8 = (f32[4,384]{1,0:T(4,128)S(1)}, f32[4,384]{1,0:T(4,128)S(1)}, u32[]{:S(2)}, u32[]{:S(2)}) collective-permute-start(f32[4,384]{1,0:T(4,128)S(1)} %slice.37), channel_id=1, source_target_pairs={{0,10},{1,11},{2,8},{3,9},{4,14},{5,15},{6,12},{7,13},{8,2},{9,3},... | collective-permute-start | bytes 18440 | tf_op jit(solution)/shard_map/ppermute | solution.py:177
  29.4 3.1 %collective-permute-start.9 = (f32[2,384]{1,0:T(2,128)S(1)}, f32[2,384]{1,0:T(2,128)S(1)}, u32[]{:S(2)}, u32[]{:S(2)}) collective-permute-start(f32[2,384]{1,0:T(2,128)S(1)} %slice.39), channel_id=1, source_target_pairs={{0,9},{1,8},{2,11},{3,10},{4,13},{5,12},{6,15},{7,14},{8,1},{9,0},... | collective-permute-start | bytes 9224 | tf_op jit(solution)/shard_map/ppermute | solution.py:177

commit v3 on v2

--- a/solution.py
+++ b/solution.py
@@ -10,6 +10,7 @@
 
 EPSILON = 1e-05
 LANES = 128
+FIRST = 4
 BF16 = jnp.bfloat16
 F32 = jnp.float32
 
@@ -22,85 +23,115 @@
 
 
 def filter_kernel(
-    batch,
     own_classes,
     classes,
     groups_ref,
     best_ref,
-    images_ref,
-    row_ref,
-    column_ref,
-    mask_ref,
+    images_hbm,
+    row_hbm,
+    column_hbm,
+    mask_hbm,
     basis_rows_ref,
     basis_columns_ref,
     assignments_ref,
     sharp_ref,
     out_ref,
+    images_ref,
+    row_ref,
+    column_ref,
+    mask_ref,
     inner,
+    sems,
 ):
-    step = pl.program_id(0)
     pixels = mask_ref.shape[0]
     row_count = basis_rows_ref.shape[0]
     column_count = basis_columns_ref.shape[0]
     width = row_count * column_count
     particles, message = out_ref.shape
 
-    group = [groups_ref[step * batch + b] for b in range(batch)]
-    half = [
-        jnp.dot(images_ref[b], column_ref[group[b]], preferred_element_type=F32).astype(BF16)
-        for b in range(batch)
+    first = min(FIRST, particles)
+    spans = [(0, first), (first, particles - first)]
+    fetch_column = pltpu.make_async_copy(column_hbm, column_ref, sems.at[0])
+    fetch_row = pltpu.make_async_copy(row_hbm, row_ref, sems.at[1])
+    fetch_mask = pltpu.make_async_copy(mask_hbm, mask_ref, sems.at[2])
+    fetch_images = [
+        pltpu.make_async_copy(
+            images_hbm.at[start : start + size], images_ref.at[start : start + size], sems.at[3 + i]
+        )
+        for i, (start, size) in enumerate(spans)
+        if size
     ]
-    scale = []
-    masked = []
-    for b in range(batch):
-        filtered = jnp.dot(row_ref[group[b]], half[b], preferred_element_type=F32) * mask_ref[...]
-        power = jnp.sum(filtered * filtered, axis=0, keepdims=True)
-        power = jnp.sum(power, axis=1, keepdims=True) * (1.0 / (pixels * pixels))
-        scale.append(lax.rsqrt(power + EPSILON))
-        masked.append(filtered.astype(BF16))
-    for b in range(batch):
-        rows = jnp.dot(basis_rows_ref[...], masked[b], preferred_element_type=F32)
-        place = pl.multiple_of((step * batch + b) * row_count, row_count)
-        inner[pl.ds(place, row_count), :] = rows * scale[b]
-
-    @pl.when(step == pl.num_programs(0) - 1)
-    def _():
-        lane = lax.broadcasted_iota(jnp.int32, (column_count, width), 1)
-        which = lax.broadcasted_iota(jnp.int32, (column_count, width), 0)
-        spread = (lane % column_count == which).astype(F32).astype(BF16)
-        wide = lax.dot_general(
-            basis_columns_ref[...], spread, (((0,), (0,)), ((), ())), preferred_element_type=F32
-        ).astype(BF16)
-        held = inner[...]
-        high = held.astype(BF16)
-        low = (held - high.astype(F32)).astype(BF16)
-        both = jnp.dot(high, wide, preferred_element_type=F32)
-        both = both + jnp.dot(low, wide, preferred_element_type=F32)
-        lane = lax.broadcasted_iota(jnp.int32, both.shape, 1)
-        which = lax.broadcasted_iota(jnp.int32, both.shape, 0)
-        both = jnp.where(lane // column_count == which % row_count, both, 0.0)
-        coeffs = jnp.sum(both.reshape(particles, row_count, width), axis=1)
-
-        lane = lax.broadcasted_iota(jnp.int32, (particles, message - width), 1)
-        place = lax.broadcasted_iota(jnp.int32, (particles, message - width), 0)
-        named = (lane // own_classes ^ lax.axis_index("cls")) * own_classes + lane % own_classes
-        named = jnp.where(lane < classes, named, -1)
-        meta = jnp.zeros(lane.shape, F32)
-        assignments = assignments_ref[...]
-        for j in range(assignments.shape[1]):
-            meta = jnp.where(assignments[:, j : j + 1] == named, 1.0, meta)
-        square = (particles, particles)
-        same = lax.broadcasted_iota(jnp.int32, square, 0) == lax.broadcasted_iota(
-            jnp.int32, square, 1
+    fetch_column.start()
+    fetch_images[0].start()
+    fetch_row.start()
+    fetch_mask.start()
+    for fetch in fetch_images[1:]:
+        fetch.start()
+
+    lane = lax.broadcasted_iota(jnp.int32, (column_count, width), 1)
+    which = lax.broadcasted_iota(jnp.int32, (column_count, width), 0)
+    spread = (lane % column_count == which).astype(F32).astype(BF16)
+    wide = lax.dot_general(
+        basis_columns_ref[...], spread, (((0,), (0,)), ((), ())), preferred_element_type=F32
+    ).astype(BF16)
+    lane = lax.broadcasted_iota(jnp.int32, (particles, message - width), 1)
+    place = lax.broadcasted_iota(jnp.int32, (particles, message - width), 0)
+    named = (lane // own_classes ^ lax.axis_index("cls")) * own_classes + lane % own_classes
+    named = jnp.where(lane < classes, named, -1)
+    meta = jnp.zeros(lane.shape, F32)
+    assignments = assignments_ref[...]
+    for j in range(assignments.shape[1]):
+        meta = jnp.where(assignments[:, j : j + 1] == named, 1.0, meta)
+    square = (particles, particles)
+    same = lax.broadcasted_iota(jnp.int32, square, 0) == lax.broadcasted_iota(
+        jnp.int32, square, 1
+    )
+    sharp = jnp.broadcast_to(sharp_ref[...].astype(F32), square)
+    sharp = jnp.sum(jnp.where(same, sharp, 0.0), axis=1, keepdims=True)
+    meta = jnp.where(lane == classes, sharp, meta)
+    for n in range(particles):
+        meta = jnp.where(
+            (place == n) & (lane == classes + 1), best_ref[n].astype(F32), meta
         )
-        sharp = jnp.broadcast_to(sharp_ref[...].astype(F32), square)
-        sharp = jnp.sum(jnp.where(same, sharp, 0.0), axis=1, keepdims=True)
-        meta = jnp.where(lane == classes, sharp, meta)
-        for n in range(particles):
-            meta = jnp.where(
-                (place == n) & (lane == classes + 1), best_ref[n].astype(F32), meta
-            )
-        out_ref[...] = jnp.concatenate([coeffs.astype(BF16), meta.astype(BF16)], axis=1)
+
+    for i, fetch in enumerate(fetch_images):
+        start, size = spans[i]
+        each = range(start, start + size)
+        if i == 0:
+            fetch_column.wait()
+        fetch.wait()
+        half = {
+            n: jnp.dot(
+                images_ref[n], column_ref[groups_ref[n]], preferred_element_type=F32
+            ).astype(BF16)
+            for n in each
+        }
+        if i == 0:
+            fetch_row.wait()
+            fetch_mask.wait()
+        scale, masked = {}, {}
+        for n in each:
+            filtered = jnp.dot(row_ref[groups_ref[n]], half[n], preferred_element_type=F32)
+            filtered = filtered * mask_ref[...]
+            power = jnp.sum(filtered * filtered, axis=0, keepdims=True)
+            power = jnp.sum(power, axis=1, keepdims=True) * (1.0 / (pixels * pixels))
+            scale[n] = lax.rsqrt(power + EPSILON)
+            masked[n] = filtered.astype(BF16)
+        for n in each:
+            rows = jnp.dot(basis_rows_ref[...], masked[n], preferred_element_type=F32)
+            inner[n * row_count : (n + 1) * row_count, :] = rows * scale[n]
+
+    held = inner[...]
+    high = held.astype(BF16)
+    low = (held - high.astype(F32)).astype(BF16)
+    both = jnp.dot(high, wide, preferred_element_type=F32)
+    both = both + jnp.dot(low, wide, preferred_element_type=F32)
+    lane = lax.broadcasted_iota(jnp.int32, both.shape, 1)
+    which = lax.broadcasted_iota(jnp.int32, both.shape, 0)
+    both = jnp.where(lane // column_count == which % row_count, both, 0.0)
+    coeffs = jnp.sum(both.reshape(particles, row_count, width), axis=1)
+
+    out_ref[...] = jnp.concatenate([coeffs.astype(BF16), meta.astype(BF16)], axis=1)
 
 
 def filter_images(
@@ -121,32 +152,23 @@
     row_count, column_count = basis_rows.shape[1], basis_columns.shape[1]
     message = row_count * column_count + classes + 2
     message += -message % LANES
-    batch = 8 if particles % 8 == 0 else 1
     mask = jnp.asarray(soft_edge(pixels))
-    whole2 = lambda s, *_: (0, 0)
-    whole3 = lambda s, *_: (0, 0, 0)
+    anywhere = pl.BlockSpec(memory_space=pl.ANY)
+    whole = pl.BlockSpec(memory_space=pltpu.VMEM)
     return pl.pallas_call(
-        lambda *refs: filter_kernel(batch, own_classes, classes, *refs),
+        lambda *refs: filter_kernel(own_classes, classes, *refs),
         out_shape=pltpu.VMEM((particles, message), BF16),
-        grid_spec=pltpu.PrefetchScalarGridSpec(
-            num_scalar_prefetch=2,
-            grid=(particles // batch,),
-            in_specs=[
-                pl.BlockSpec((batch, pixels, pixels), lambda s, *_: (s, 0, 0)),
-                pl.BlockSpec((groups, pixels, pixels), whole3),
-                pl.BlockSpec((groups, pixels, pixels), whole3),
-                pl.BlockSpec((pixels, pixels), whole2),
-                pl.BlockSpec((row_count, pixels), whole2),
-                pl.BlockSpec((column_count, pixels), whole2),
-                pl.BlockSpec(assignments.shape, whole2),
-                pl.BlockSpec((1, particles), whole2),
-            ],
-            out_specs=pl.BlockSpec((particles, message), whole2),
-            scratch_shapes=[pltpu.VMEM((particles * row_count, pixels), F32)],
-        ),
-        compiler_params=pltpu.CompilerParams(
-            dimension_semantics=("arbitrary",), vmem_limit_bytes=60 * 1024 * 1024
-        ),
+        in_specs=[pl.BlockSpec(memory_space=pltpu.SMEM)] * 2 + [anywhere] * 4 + [whole] * 4,
+        out_specs=whole,
+        scratch_shapes=[
+            pltpu.VMEM(images.shape, BF16),
+            pltpu.VMEM(row_filters.shape, BF16),
+            pltpu.VMEM(column_filters.shape, BF16),
+            pltpu.VMEM((pixels, pixels), F32),
+            pltpu.VMEM((particles * row_count, pixels), F32),
+            pltpu.SemaphoreType.DMA((5,)),
+        ],
+        compiler_params=pltpu.CompilerParams(vmem_limit_bytes=60 * 1024 * 1024),
         cost_estimate=pl.CostEstimate(
             flops=4 * particles * pixels**3,
             bytes_accessed=2 * pixels * pixels * (particles + 2 * groups),
@@ -234,7 +256,7 @@
 
     q, k = iotas((classes, sections * spare))
     row = k % spare
-    place = (k // spare ^ section) + row // own_classes * sections
+    place = (k // spare ^ section ^ sections - 1) + row // own_classes * sections
     place = place * own_classes + row % own_classes
     fetched = classes // sections
     refs = jnp.dot(
@@ -338,13 +360,13 @@
     refs = []
     for first in range(0, min(owners, 2 * sections), sections):
         pairs = [
-            (s * owners + c, s * owners + (c ^ (first + s or 1)))
+            (s * owners + c, s * owners + (c ^ (first + sections - 1 - s or 1)))
             for s in range(sections)
             for c in range(owners)
         ]
         block = lax.ppermute(references, ("section", "cls"), pairs)
         if first == 0:
-            block = jnp.where(lax.axis_index("section") == 0, references, block)
+            block = jnp.where(lax.axis_index("section") == sections - 1, references, block)
         refs.append(block)
     refs = jnp.concatenate(refs, axis=0)
     distance = 2 * sections

time: 33.2 us -> 32.3 us (0.973)
  waiting for transfers between devices: 16.5 us -> 12 us
  starting transfers between devices: 8.15 us -> 11.9 us
    ppermute x3, starting transfers between devices: 0.31 us -> 2.93 us  [cross(): return lax.ppermute(array, ('section', 'cls'), pairs)]
    ppermute x3, waiting for transfers between devices: 9.41 us -> 6.9 us  [cross(): return lax.ppermute(array, ('section', 'cls'), pairs)]
    ppermute x5, waiting for transfers between devices: 7.05 us -> 5.11 us  [swap(): return lax.ppermute(array, axis, [(i, i ^ distance) for i in range(size)])]
    ppermute x2, starting transfers between devices: 5.18 us -> 6.02 us  [body(): block = lax.ppermute(references, ('section', 'cls'), pairs)]
where the time goes in v3:
time: 32.3 us; the launch traced here: 32.1 us
  waiting for transfers between devices  12 us (37%)
  starting transfers between devices  11.9 us (37%)
  Pallas kernels  6.29 us (19%)
  between operations  0.72 us (2%)
  other arithmetic  0.63 us (2%)
  local copies, waits for them, and re-layouts  0.54 us (2%)
    ppermute x3, waiting for transfers between devices, cross(): return lax.ppermute(array, ('section', 'cls'), pairs)  6.9 us
    ppermute x2, starting transfers between devices, body(): block = lax.ppermute(references, ('section', 'cls'), pairs)  6.02 us
    ppermute x5, waiting for transfers between devices, swap(): return lax.ppermute(array, axis, [(i, i ^ distance) for i in range(size)])  5.11 us
    pallas_call x1, Pallas kernels, filter_images(): pl.pallas_call(lambda *refs: filter_kernel(own_classes, classes, *refs),...  4.41 us
    ppermute x5, starting transfers between devices, swap(): return lax.ppermute(array, axis, [(i, i ^ distance) for i in range(size)])  2.97 us
    ppermute x3, starting transfers between devices, cross(): return lax.ppermute(array, ('section', 'cls'), pairs)  2.93 us
    pallas_call x2, Pallas kernels, small_call(): pl.pallas_call(kernel, out_shape=out_shape, in_specs=[pl.BlockSpec(memory...  1.88 us
  transfers between devices with their start and end apart: 10, of which 6 were waited for; matrix products, arithmetic and copies ran while one was open for 2% of the time, Pallas kernels for 14%

profile of v3, /device:TPU:0, one launch (start us, length us, event | category | flops | bytes accessed | tf_op | source)
XLA Modules:
  0.0 32.1 jit_solution(16293311831162519010)
XLA Ops:
  0.6 0.5 %collective-permute-start.5 = (bf16[9,256,256]{2,1,0:T(8,128)(2,1)}, bf16[9,256,256]{2,1,0:T(8,128)(2,1)S(1)}, u32[]{:S(2)}, u32[]{:S(2)}) collective-permute-start(bf16[9,256,256]{2,1,0:T(8,128)(2,1)} %r_4_.1), channel_id=1, source_target_pairs={{0,8},{8,0},{16,24},{24,16},{1,9},{9,1},{17,25},{25,17},{2,10},{10... | collective-permute-start | bytes 3538952 | tf_op jit(solution)/shard_map/ppermute | solution.py:204
  1.2 3.6 %collective-permute-start = (bf16[2,256]{1,0:T(2,128)(2,1)}, bf16[2,256]{1,0:T(2,128)(2,1)S(1)}, u32[]{:S(2)}, u32[]{:S(2)}) collective-permute-start(bf16[2,256]{1,0:T(2,128)(2,1)} %param.19), channel_id=1, source_target_pairs={{0,3},{1,2},{2,1},{3,0},{4,7},{5,6},{6,5},{7,4},{8,10},{9,11},{10,... | collective-permute-start | bytes 3080 | tf_op jit(solution)/shard_map/ppermute | solution.py:367
  4.8 2.4 %collective-permute-start.1 = (bf16[2,256]{1,0:T(2,128)(2,1)}, bf16[2,256]{1,0:T(2,128)(2,1)S(1)}, u32[]{:S(2)}, u32[]{:S(2)}) collective-permute-start(bf16[2,256]{1,0:T(2,128)(2,1)} %param.19), channel_id=1, source_target_pairs={{0,7},{1,6},{2,5},{3,4},{4,3},{5,2},{6,1},{7,0},{8,14},{9,15},{10,... | collective-permute-start | bytes 3080 | tf_op jit(solution)/shard_map/ppermute | solution.py:367
  7.2 4.4 %filter_images.1 = bf16[16,384]{1,0:T(8,128)(2,1)S(1)} custom-call(s32[16]{0:T(128)} %refs_0_.1, s32[16]{0:T(128)} %refs_1_.1, bf16[16,256,256]{2,1,0:T(8,128)(2,1)} %refs_2_.1, bf16[4,256,256]{2,1,0:T(8,128)(2,1)} %refs_3_.1, bf16[4,256,256]{2,1,0:T(8,128)(2,1)} %refs_4_.1, f32[256,256]{1,0:T(8,128)} %constant.14.clone.refs_5_, bf16[16,256]{1,0:T(8,128)(2,1)} %bitcast.5, ...), custom_call_target="tpu_custom_call" | custom-call | flops 1073741824 | bytes 3145728 | tf_op jit(solution)/shard_map/filter_images/pallas_call | solution.py:158
  11.6 0.0 collective-permute-done
  11.7 0.2 collective-permute-start.4
  11.9 0.5 %collective-permute-start.3 = (bf16[32,384]{1,0:T(8,128)(2,1)S(1)}, bf16[32,384]{1,0:T(8,128)(2,1)S(1)}, u32[]{:S(2)}, u32[]{:S(2)}) collective-permute-start(bf16[32,384]{1,0:T(8,128)(2,1)S(1)} %pad_maximum_fusion.r_0_), channel_id=1, source_target_pairs={{0,16},{8,24},{16,0},{24,8},{1,17},{9,25},{17,1},{25,9},{2,18},{10... | collective-permute-start | bytes 73736 | tf_op jit(solution)/shard_map/ppermute | solution.py:204
  12.4 1.2 %collective-permute-start.2 = (bf16[32,384]{1,0:T(8,128)(2,1)S(1)}, bf16[32,384]{1,0:T(8,128)(2,1)S(1)}, u32[]{:S(2)}, u32[]{:S(2)}) collective-permute-start(bf16[32,384]{1,0:T(8,128)(2,1)S(1)} %pad_maximum_fusion.r_0_), channel_id=1, source_target_pairs={{0,8},{8,0},{16,24},{24,16},{1,9},{9,1},{17,25},{25,17},{2,10},{10... | collective-permute-start | bytes 73736 | tf_op jit(solution)/shard_map/ppermute | solution.py:204
  13.6 1.4 %collective-permute-done.4.r_3_ = bf16[32,384]{1,0:T(8,128)(2,1)S(1)} collective-permute-done((bf16[32,384]{1,0:T(8,128)(2,1)S(1)}, bf16[32,384]{1,0:T(8,128)(2,1)S(1)}, u32[]{:S(2)}, u32[]{:S(2)}) %collective-permute-start.4) | collective-permute-done | bytes 24608 | tf_op jit(solution)/shard_map/ppermute | solution.py:204
  15.0 0.7 %collective-permute-done.3.r_2_ = bf16[32,384]{1,0:T(8,128)(2,1)S(1)} collective-permute-done((bf16[32,384]{1,0:T(8,128)(2,1)S(1)}, bf16[32,384]{1,0:T(8,128)(2,1)S(1)}, u32[]{:S(2)}, u32[]{:S(2)}) %collective-permute-start.3) | collective-permute-done | bytes 24608 | tf_op jit(solution)/shard_map/ppermute | solution.py:204
  15.7 0.0 collective-permute-done.2.r_1_
  15.7 0.0 collective-permute-done.5.r_5_
  15.7 1.5 %scores.1 = (bf16[80,256]{1,0:T(8,128)(2,1)S(1)}, f32[16,64]{1,0:T(8,128)S(1)}) custom-call(bf16[32,384]{1,0:T(8,128)(2,1)S(1)} %pad_maximum_fusion.r_0_, bf16[32,384]{1,0:T(8,128)(2,1)S(1)} %collective-permute-done.2.r_1_, bf16[32,384]{1,0:T(8,128)(2,1)S(1)} %collective-permute-done.3.r_2_, bf16[32,384]{1,0:T(8,128)(2,1)S(1)} %collective-permute-done.4.r_3_, ...), custom_call_target="tpu_custom_call" | custom-call | bytes 2457600 | tf_op jit(solution)/shard_map/scores/pallas_call | solution.py:327
  17.2 0.5 %collective-permute-start.6 = (bf16[80,256]{1,0:T(8,128)(2,1)S(1)}, bf16[80,256]{1,0:T(8,128)(2,1)S(1)}, u32[]{:S(2)}, u32[]{:S(2)}) collective-permute-start(bf16[80,256]{1,0:T(8,128)(2,1)S(1)} %get-tuple-element.6.r_0_), channel_id=1, source_target_pairs={{0,24},{8,16},{16,8},{24,0},{1,25},{9,17},{17,9},{25,1},{2,26},{10... | collective-permute-start | bytes 122888 | tf_op jit(solution)/shard_map/ppermute | solution.py:204
  17.7 3.0 %collective-permute-done.6.r_1_ = bf16[80,256]{1,0:T(8,128)(2,1)S(1)} collective-permute-done((bf16[80,256]{1,0:T(8,128)(2,1)S(1)}, bf16[80,256]{1,0:T(8,128)(2,1)S(1)}, u32[]{:S(2)}, u32[]{:S(2)}) %collective-permute-start.6) | collective-permute-done | bytes 40992 | tf_op jit(solution)/shard_map/ppermute | solution.py:204
  20.7 0.4 %class_sums.1 = (f32[16,384]{1,0:T(8,128)S(1)}, f32[1,64]{1,0:T(1,128)S(1)}) custom-call(bf16[80,256]{1,0:T(8,128)(2,1)S(1)} %get-tuple-element.6.r_0_, bf16[80,256]{1,0:T(8,128)(2,1)S(1)} %collective-permute-done.6.r_1_, f32[16,64]{1,0:T(8,128)S(1)} %get-tuple-element.7.r_2_), custom_call_target="tpu_custom_call" | custom-call | bytes 86016 | tf_op jit(solution)/shard_map/class_sums/pallas_call | solution.py:327
  21.1 0.2 collective-permute-start.7
  21.3 4.0 %collective-permute-done.7 = f32[8,384]{1,0:T(8,128)S(1)} collective-permute-done((f32[8,384]{1,0:T(8,128)S(1)}, f32[8,384]{1,0:T(8,128)S(1)}, u32[]{:S(2)}, u32[]{:S(2)}) %collective-permute-start.7) | collective-permute-done | bytes 12320 | tf_op jit(solution)/shard_map/ppermute | solution.py:199
  25.3 1.3 %collective-permute-start.8 = (f32[4,384]{1,0:T(4,128)S(1)}, f32[4,384]{1,0:T(4,128)S(1)}, u32[]{:S(2)}, u32[]{:S(2)}) collective-permute-start(f32[4,384]{1,0:T(4,128)S(1)} %slice.37), channel_id=1, source_target_pairs={{0,10},{1,11},{2,8},{3,9},{4,14},{5,15},{6,12},{7,13},{8,2},{9,3},... | collective-permute-start | bytes 18440 | tf_op jit(solution)/shard_map/ppermute | solution.py:199
  26.6 1.8 %collective-permute-done.8 = f32[4,384]{1,0:T(4,128)S(1)} collective-permute-done((f32[4,384]{1,0:T(4,128)S(1)}, f32[4,384]{1,0:T(4,128)S(1)}, u32[]{:S(2)}, u32[]{:S(2)}) %collective-permute-start.8) | collective-permute-done | bytes 6176 | tf_op jit(solution)/shard_map/ppermute | solution.py:199
  28.4 1.4 %collective-permute-start.9 = (f32[2,384]{1,0:T(2,128)S(1)}, f32[2,384]{1,0:T(2,128)S(1)}, u32[]{:S(2)}, u32[]{:S(2)}) collective-permute-start(f32[2,384]{1,0:T(2,128)S(1)} %slice.39), channel_id=1, source_target_pairs={{0,9},{1,8},{2,11},{3,10},{4,13},{5,12},{6,15},{7,14},{8,1},{9,0},... | collective-permute-start | bytes 9224 | tf_op jit(solution)/shard_map/ppermute | solution.py:199
  29.8 0.5 %slice_bitcast_fusion = f32[16]{0:T(128)} fusion(f32[1,64]{1,0:T(1,128)S(1)} %get-tuple-element.9), kind=kLoop, calls=%fused_computation.16 | loop fusion | bytes 128 | tf_op jit(solution)/shard_map/squeeze | solution.py:424
  30.4 1.2 %collective-permute-done.9 = f32[2,384]{1,0:T(2,128)S(1)} collective-permute-done((f32[2,384]{1,0:T(2,128)S(1)}, f32[2,384]{1,0:T(2,128)S(1)}, u32[]{:S(2)}, u32[]{:S(2)}) %collective-permute-start.9) | collective-permute-done | bytes 3104 | tf_op jit(solution)/shard_map/ppermute | solution.py:199
  31.5 0.6 %fusion.6 = f32[2,256]{1,0:T(2,128)} fusion(f32[2,384]{1,0:T(2,128)S(1)} %slice_add_fusion.2, f32[2,128]{1,0:T(2,128)S(1)} %slice.41, bf16[2,256]{1,0:T(2,128)(2,1)S(1)} %copy-done.1), kind=kLoop, calls=%fused_computation.13 | loop fusion | flops 2560 | bytes 6144 | tf_op jit(solution)/shard_map/div | solution.py:423
  (15 shorter events, 0.1 us)
Async XLA Ops:
  0.6 15.1 %collective-permute-start.5 = (bf16[9,256,256]{2,1,0:T(8,128)(2,1)}, bf16[9,256,256]{2,1,0:T(8,128)(2,1)S(1)}, u32[]{:S(2)}, u32[]{:S(2)}) collective-permute-start(bf16[9,256,256]{2,1,0:T(8,128)(2,1)} %r_4_.1), channel_id=1, source_target_pairs={{0,8},{8,0},{16,24},{24,16},{1,9},{9,1},{17,25},{25,17},{2,10},{10... | collective-permute-start | bytes 3538952 | tf_op jit(solution)/shard_map/ppermute | solution.py:204
  1.2 10.5 %collective-permute-start = (bf16[2,256]{1,0:T(2,128)(2,1)}, bf16[2,256]{1,0:T(2,128)(2,1)S(1)}, u32[]{:S(2)}, u32[]{:S(2)}) collective-permute-start(bf16[2,256]{1,0:T(2,128)(2,1)} %param.19), channel_id=1, source_target_pairs={{0,3},{1,2},{2,1},{3,0},{4,7},{5,6},{6,5},{7,4},{8,10},{9,11},{10,... | collective-permute-start | bytes 3080 | tf_op jit(solution)/shard_map/ppermute | solution.py:367
  4.8 6.9 %collective-permute-start.1 = (bf16[2,256]{1,0:T(2,128)(2,1)}, bf16[2,256]{1,0:T(2,128)(2,1)S(1)}, u32[]{:S(2)}, u32[]{:S(2)}) collective-permute-start(bf16[2,256]{1,0:T(2,128)(2,1)} %param.19), channel_id=1, source_target_pairs={{0,7},{1,6},{2,5},{3,4},{4,3},{5,2},{6,1},{7,0},{8,14},{9,15},{10,... | collective-permute-start | bytes 3080 | tf_op jit(solution)/shard_map/ppermute | solution.py:367
  7.2 4.4 %copy-start.1 = (bf16[2,256]{1,0:T(2,128)(2,1)S(1)}, bf16[2,256]{1,0:T(2,128)(2,1)}, u32[]{:S(2)}) copy-start(bf16[2,256]{1,0:T(2,128)(2,1)} %param.19) | copy-start | bytes 3076
  7.2 8.5 %copy-start = (bf16[9,256,256]{2,1,0:T(8,128)(2,1)S(1)}, bf16[9,256,256]{2,1,0:T(8,128)(2,1)}, u32[]{:S(2)}) copy-start(bf16[9,256,256]{2,1,0:T(8,128)(2,1)} %r_4_.1) | copy-start | bytes 3538948
  11.7 3.3 %collective-permute-start.4 = (bf16[32,384]{1,0:T(8,128)(2,1)S(1)}, bf16[32,384]{1,0:T(8,128)(2,1)S(1)}, u32[]{:S(2)}, u32[]{:S(2)}) collective-permute-start(bf16[32,384]{1,0:T(8,128)(2,1)S(1)} %pad_maximum_fusion.r_0_), channel_id=1, source_target_pairs={{0,24},{8,16},{16,8},{24,0},{1,25},{9,17},{17,9},{25,1},{2,26},{10... | collective-permute-start | bytes 73736 | tf_op jit(solution)/shard_map/ppermute | solution.py:204
  11.9 3.8 %collective-permute-start.3 = (bf16[32,384]{1,0:T(8,128)(2,1)S(1)}, bf16[32,384]{1,0:T(8,128)(2,1)S(1)}, u32[]{:S(2)}, u32[]{:S(2)}) collective-permute-start(bf16[32,384]{1,0:T(8,128)(2,1)S(1)} %pad_maximum_fusion.r_0_), channel_id=1, source_target_pairs={{0,16},{8,24},{16,0},{24,8},{1,17},{9,25},{17,1},{25,9},{2,18},{10... | collective-permute-start | bytes 73736 | tf_op jit(solution)/shard_map/ppermute | solution.py:204
  12.4 3.3 %collective-permute-start.2 = (bf16[32,384]{1,0:T(8,128)(2,1)S(1)}, bf16[32,384]{1,0:T(8,128)(2,1)S(1)}, u32[]{:S(2)}, u32[]{:S(2)}) collective-permute-start(bf16[32,384]{1,0:T(8,128)(2,1)S(1)} %pad_maximum_fusion.r_0_), channel_id=1, source_target_pairs={{0,8},{8,0},{16,24},{24,16},{1,9},{9,1},{17,25},{25,17},{2,10},{10... | collective-permute-start | bytes 73736 | tf_op jit(solution)/shard_map/ppermute | solution.py:204
  17.2 3.5 %collective-permute-start.6 = (bf16[80,256]{1,0:T(8,128)(2,1)S(1)}, bf16[80,256]{1,0:T(8,128)(2,1)S(1)}, u32[]{:S(2)}, u32[]{:S(2)}) collective-permute-start(bf16[80,256]{1,0:T(8,128)(2,1)S(1)} %get-tuple-element.6.r_0_), channel_id=1, source_target_pairs={{0,24},{8,16},{16,8},{24,0},{1,25},{9,17},{17,9},{25,1},{2,26},{10... | collective-permute-start | bytes 122888 | tf_op jit(solution)/shard_map/ppermute | solution.py:204
  21.1 4.1 %collective-permute-start.7 = (f32[8,384]{1,0:T(8,128)S(1)}, f32[8,384]{1,0:T(8,128)S(1)}, u32[]{:S(2)}, u32[]{:S(2)}) collective-permute-start(f32[8,384]{1,0:T(8,128)S(1)} %slice.28), channel_id=1, source_target_pairs={{0,12},{1,13},{2,14},{3,15},{4,8},{5,9},{6,10},{7,11},{8,4},{9,5},... | collective-permute-start | bytes 36872 | tf_op jit(solution)/shard_map/ppermute | solution.py:199
  25.3 3.1 %collective-permute-start.8 = (f32[4,384]{1,0:T(4,128)S(1)}, f32[4,384]{1,0:T(4,128)S(1)}, u32[]{:S(2)}, u32[]{:S(2)}) collective-permute-start(f32[4,384]{1,0:T(4,128)S(1)} %slice.37), channel_id=1, source_target_pairs={{0,10},{1,11},{2,8},{3,9},{4,14},{5,15},{6,12},{7,13},{8,2},{9,3},... | collective-permute-start | bytes 18440 | tf_op jit(solution)/shard_map/ppermute | solution.py:199
  28.4 3.1 %collective-permute-start.9 = (f32[2,384]{1,0:T(2,128)S(1)}, f32[2,384]{1,0:T(2,128)S(1)}, u32[]{:S(2)}, u32[]{:S(2)}) collective-permute-start(f32[2,384]{1,0:T(2,128)S(1)} %slice.39), channel_id=1, source_target_pairs={{0,9},{1,8},{2,11},{3,10},{4,13},{5,12},{6,15},{7,14},{8,1},{9,0},... | collective-permute-start | bytes 9224 | tf_op jit(solution)/shard_map/ppermute | solution.py:199

commit v4 on v3

--- a/solution.py
+++ b/solution.py
@@ -242,9 +242,11 @@
 
 
 def score_kernel(
-    particles, sections, own_classes, classes, *refs
+    particles, order, own_classes, classes, *refs
 ):
-    messages, (own_ref, sibling_ref, out_ref, listed_ref) = refs[:sections], refs[sections:]
+    sections = len(order)
+    own_ref, sibling_ref, out_ref, listed_ref = refs[sections:]
+    messages = [refs[order.index(m)] for m in range(sections)]
     local_rotations, width, _ = own_ref.shape
     section = lax.axis_index("section")
     held = sections * particles
@@ -389,11 +391,12 @@
     )
     refs = jnp.pad(refs, ((0, -refs.shape[0] % 16), (0, message.shape[1] - width)))
     message = jnp.concatenate([message, refs], axis=0)
+    order = [*range(1, sections, 2), *range(2, sections, 2)]
     marg, listed = small_call(
-        lambda *r: score_kernel(particles, sections, own_classes, classes, *r),
+        lambda *r: score_kernel(particles, [0, *order], own_classes, classes, *r),
         "scores",
         message,
-        *[swap(message, "section", k) for k in range(1, sections)],
+        *[swap(message, "section", k) for k in order],
         rotations,
         sibling_rotations,
         out_shape=(

time: 32.3 us -> 32.4 us (level)
  waiting for transfers between devices: 12 us -> 12.4 us
    ppermute x5, waiting for transfers between devices: 5.11 us -> 5.51 us  [swap(): return lax.ppermute(array, axis, [(i, i ^ distance) for i in range(size)])]
  transfers between devices with their start and end apart: 10 -> 10, of which waited for: 6 -> 5; matrix products, arithmetic and copies ran while one was open for 2% -> 2% of each run, Pallas kernels for 14% -> 14%
where the time goes in v4:
time: 32.4 us; the launch traced here: 32.3 us
  waiting for transfers between devices  12.4 us (38%)
  starting transfers between devices  11.6 us (36%)
  Pallas kernels  6.29 us (19%)
  between operations  0.72 us (2%)
  other arithmetic  0.63 us (2%)
  local copies, waits for them, and re-layouts  0.54 us (2%)
    ppermute x3, waiting for transfers between devices, cross(): return lax.ppermute(array, ('section', 'cls'), pairs)  6.94 us
    ppermute x2, starting transfers between devices, body(): block = lax.ppermute(references, ('section', 'cls'), pairs)  6.02 us
    ppermute x5, waiting for transfers between devices, swap(): return lax.ppermute(array, axis, [(i, i ^ distance) for i in range(size)])  5.51 us
    pallas_call x1, Pallas kernels, filter_images(): pl.pallas_call(lambda *refs: filter_kernel(own_classes, classes, *refs),...  4.41 us
    ppermute x5, starting transfers between devices, swap(): return lax.ppermute(array, axis, [(i, i ^ distance) for i in range(size)])  2.82 us
    ppermute x3, starting transfers between devices, cross(): return lax.ppermute(array, ('section', 'cls'), pairs)  2.79 us
    pallas_call x2, Pallas kernels, small_call(): pl.pallas_call(kernel, out_shape=out_shape, in_specs=[pl.BlockSpec(memory...  1.88 us
  transfers between devices with their start and end apart: 10, of which 5 were waited for; matrix products, arithmetic and copies ran while one was open for 2% of the time, Pallas kernels for 14%

profile of v4, /device:TPU:0, one launch (start us, length us, event | category | flops | bytes accessed | tf_op | source)
XLA Modules:
  0.0 32.3 jit_solution(7480701479895579451)
XLA Ops:
  0.6 0.5 %collective-permute-start.5 = (bf16[9,256,256]{2,1,0:T(8,128)(2,1)}, bf16[9,256,256]{2,1,0:T(8,128)(2,1)S(1)}, u32[]{:S(2)}, u32[]{:S(2)}) collective-permute-start(bf16[9,256,256]{2,1,0:T(8,128)(2,1)} %r_4_.1), channel_id=1, source_target_pairs={{0,8},{8,0},{16,24},{24,16},{1,9},{9,1},{17,25},{25,17},{2,10},{10... | collective-permute-start | bytes 3538952 | tf_op jit(solution)/shard_map/ppermute | solution.py:204
  1.2 3.6 %collective-permute-start = (bf16[2,256]{1,0:T(2,128)(2,1)}, bf16[2,256]{1,0:T(2,128)(2,1)S(1)}, u32[]{:S(2)}, u32[]{:S(2)}) collective-permute-start(bf16[2,256]{1,0:T(2,128)(2,1)} %param.19), channel_id=1, source_target_pairs={{0,3},{1,2},{2,1},{3,0},{4,7},{5,6},{6,5},{7,4},{8,10},{9,11},{10,... | collective-permute-start | bytes 3080 | tf_op jit(solution)/shard_map/ppermute | solution.py:369
  4.8 2.4 %collective-permute-start.1 = (bf16[2,256]{1,0:T(2,128)(2,1)}, bf16[2,256]{1,0:T(2,128)(2,1)S(1)}, u32[]{:S(2)}, u32[]{:S(2)}) collective-permute-start(bf16[2,256]{1,0:T(2,128)(2,1)} %param.19), channel_id=1, source_target_pairs={{0,7},{1,6},{2,5},{3,4},{4,3},{5,2},{6,1},{7,0},{8,14},{9,15},{10,... | collective-permute-start | bytes 3080 | tf_op jit(solution)/shard_map/ppermute | solution.py:369
  7.2 4.4 %filter_images.1 = bf16[16,384]{1,0:T(8,128)(2,1)S(1)} custom-call(s32[16]{0:T(128)} %refs_0_.1, s32[16]{0:T(128)} %refs_1_.1, bf16[16,256,256]{2,1,0:T(8,128)(2,1)} %refs_2_.1, bf16[4,256,256]{2,1,0:T(8,128)(2,1)} %refs_3_.1, bf16[4,256,256]{2,1,0:T(8,128)(2,1)} %refs_4_.1, f32[256,256]{1,0:T(8,128)} %constant.14.clone.refs_5_, bf16[16,256]{1,0:T(8,128)(2,1)} %bitcast.5, ...), custom_call_target="tpu_custom_call" | custom-call | flops 1073741824 | bytes 3145728 | tf_op jit(solution)/shard_map/filter_images/pallas_call | solution.py:158
  11.6 0.0 collective-permute-done
  11.6 0.0 collective-permute-done.1
  11.7 0.7 %collective-permute-start.4 = (bf16[32,384]{1,0:T(8,128)(2,1)S(1)}, bf16[32,384]{1,0:T(8,128)(2,1)S(1)}, u32[]{:S(2)}, u32[]{:S(2)}) collective-permute-start(bf16[32,384]{1,0:T(8,128)(2,1)S(1)} %pad_maximum_fusion.r_0_), channel_id=1, source_target_pairs={{0,16},{8,24},{16,0},{24,8},{1,17},{9,25},{17,1},{25,9},{2,18},{10... | collective-permute-start | bytes 73736 | tf_op jit(solution)/shard_map/ppermute | solution.py:204
  12.3 1.5 %collective-permute-start.2 = (bf16[32,384]{1,0:T(8,128)(2,1)S(1)}, bf16[32,384]{1,0:T(8,128)(2,1)S(1)}, u32[]{:S(2)}, u32[]{:S(2)}) collective-permute-start(bf16[32,384]{1,0:T(8,128)(2,1)S(1)} %pad_maximum_fusion.r_0_), channel_id=1, source_target_pairs={{0,8},{8,0},{16,24},{24,16},{1,9},{9,1},{17,25},{25,17},{2,10},{10... | collective-permute-start | bytes 73736 | tf_op jit(solution)/shard_map/ppermute | solution.py:204
  13.9 1.9 %collective-permute-done.4.r_3_ = bf16[32,384]{1,0:T(8,128)(2,1)S(1)} collective-permute-done((bf16[32,384]{1,0:T(8,128)(2,1)S(1)}, bf16[32,384]{1,0:T(8,128)(2,1)S(1)}, u32[]{:S(2)}, u32[]{:S(2)}) %collective-permute-start.4) | collective-permute-done | bytes 24608 | tf_op jit(solution)/shard_map/ppermute | solution.py:204
  15.8 0.0 collective-permute-done.3.r_2_
  15.8 0.0 collective-permute-done.2.r_1_
  15.9 0.0 collective-permute-done.5.r_5_
  15.9 1.5 %scores.1 = (bf16[80,256]{1,0:T(8,128)(2,1)S(1)}, f32[16,64]{1,0:T(8,128)S(1)}) custom-call(bf16[32,384]{1,0:T(8,128)(2,1)S(1)} %pad_maximum_fusion.r_0_, bf16[32,384]{1,0:T(8,128)(2,1)S(1)} %collective-permute-done.2.r_1_, bf16[32,384]{1,0:T(8,128)(2,1)S(1)} %collective-permute-done.3.r_2_, bf16[32,384]{1,0:T(8,128)(2,1)S(1)} %collective-permute-done.4.r_3_, ...), custom_call_target="tpu_custom_call" | custom-call | bytes 2457600 | tf_op jit(solution)/shard_map/scores/pallas_call | solution.py:329
  17.3 0.1 collective-permute-start.6
  17.4 3.5 %collective-permute-done.6.r_1_ = bf16[80,256]{1,0:T(8,128)(2,1)S(1)} collective-permute-done((bf16[80,256]{1,0:T(8,128)(2,1)S(1)}, bf16[80,256]{1,0:T(8,128)(2,1)S(1)}, u32[]{:S(2)}, u32[]{:S(2)}) %collective-permute-start.6) | collective-permute-done | bytes 40992 | tf_op jit(solution)/shard_map/ppermute | solution.py:204
  21.0 0.4 %class_sums.1 = (f32[16,384]{1,0:T(8,128)S(1)}, f32[1,64]{1,0:T(1,128)S(1)}) custom-call(bf16[80,256]{1,0:T(8,128)(2,1)S(1)} %get-tuple-element.6.r_0_, bf16[80,256]{1,0:T(8,128)(2,1)S(1)} %collective-permute-done.6.r_1_, f32[16,64]{1,0:T(8,128)S(1)} %get-tuple-element.7.r_2_), custom_call_target="tpu_custom_call" | custom-call | bytes 86016 | tf_op jit(solution)/shard_map/class_sums/pallas_call | solution.py:329
  21.4 0.0 collective-permute-start.7
  21.4 4.0 %collective-permute-done.7 = f32[8,384]{1,0:T(8,128)S(1)} collective-permute-done((f32[8,384]{1,0:T(8,128)S(1)}, f32[8,384]{1,0:T(8,128)S(1)}, u32[]{:S(2)}, u32[]{:S(2)}) %collective-permute-start.7) | collective-permute-done | bytes 12320 | tf_op jit(solution)/shard_map/ppermute | solution.py:199
  25.4 1.4 %collective-permute-start.8 = (f32[4,384]{1,0:T(4,128)S(1)}, f32[4,384]{1,0:T(4,128)S(1)}, u32[]{:S(2)}, u32[]{:S(2)}) collective-permute-start(f32[4,384]{1,0:T(4,128)S(1)} %slice.37), channel_id=1, source_target_pairs={{0,10},{1,11},{2,8},{3,9},{4,14},{5,15},{6,12},{7,13},{8,2},{9,3},... | collective-permute-start | bytes 18440 | tf_op jit(solution)/shard_map/ppermute | solution.py:199
  26.8 1.8 %collective-permute-done.8 = f32[4,384]{1,0:T(4,128)S(1)} collective-permute-done((f32[4,384]{1,0:T(4,128)S(1)}, f32[4,384]{1,0:T(4,128)S(1)}, u32[]{:S(2)}, u32[]{:S(2)}) %collective-permute-start.8) | collective-permute-done | bytes 6176 | tf_op jit(solution)/shard_map/ppermute | solution.py:199
  28.6 1.4 %collective-permute-start.9 = (f32[2,384]{1,0:T(2,128)S(1)}, f32[2,384]{1,0:T(2,128)S(1)}, u32[]{:S(2)}, u32[]{:S(2)}) collective-permute-start(f32[2,384]{1,0:T(2,128)S(1)} %slice.39), channel_id=1, source_target_pairs={{0,9},{1,8},{2,11},{3,10},{4,13},{5,12},{6,15},{7,14},{8,1},{9,0},... | collective-permute-start | bytes 9224 | tf_op jit(solution)/shard_map/ppermute | solution.py:199
  30.0 0.5 %slice_bitcast_fusion = f32[16]{0:T(128)} fusion(f32[1,64]{1,0:T(1,128)S(1)} %get-tuple-element.9), kind=kLoop, calls=%fused_computation.16 | loop fusion | bytes 128 | tf_op jit(solution)/shard_map/squeeze | solution.py:427
  30.5 1.2 %collective-permute-done.9 = f32[2,384]{1,0:T(2,128)S(1)} collective-permute-done((f32[2,384]{1,0:T(2,128)S(1)}, f32[2,384]{1,0:T(2,128)S(1)}, u32[]{:S(2)}, u32[]{:S(2)}) %collective-permute-start.9) | collective-permute-done | bytes 3104 | tf_op jit(solution)/shard_map/ppermute | solution.py:199
  31.7 0.6 %fusion.6 = f32[2,256]{1,0:T(2,128)} fusion(f32[2,384]{1,0:T(2,128)S(1)} %slice_add_fusion.2, f32[2,128]{1,0:T(2,128)S(1)} %slice.41, bf16[2,256]{1,0:T(2,128)(2,1)S(1)} %copy-done.1), kind=kLoop, calls=%fused_computation.13 | loop fusion | flops 2560 | bytes 6144 | tf_op jit(solution)/shard_map/div | solution.py:426
  (15 shorter events, 0.1 us)
Async XLA Ops:
  0.6 15.2 %collective-permute-start.5 = (bf16[9,256,256]{2,1,0:T(8,128)(2,1)}, bf16[9,256,256]{2,1,0:T(8,128)(2,1)S(1)}, u32[]{:S(2)}, u32[]{:S(2)}) collective-permute-start(bf16[9,256,256]{2,1,0:T(8,128)(2,1)} %r_4_.1), channel_id=1, source_target_pairs={{0,8},{8,0},{16,24},{24,16},{1,9},{9,1},{17,25},{25,17},{2,10},{10... | collective-permute-start | bytes 3538952 | tf_op jit(solution)/shard_map/ppermute | solution.py:204
  1.2 10.5 %collective-permute-start = (bf16[2,256]{1,0:T(2,128)(2,1)}, bf16[2,256]{1,0:T(2,128)(2,1)S(1)}, u32[]{:S(2)}, u32[]{:S(2)}) collective-permute-start(bf16[2,256]{1,0:T(2,128)(2,1)} %param.19), channel_id=1, source_target_pairs={{0,3},{1,2},{2,1},{3,0},{4,7},{5,6},{6,5},{7,4},{8,10},{9,11},{10,... | collective-permute-start | bytes 3080 | tf_op jit(solution)/shard_map/ppermute | solution.py:369
  4.8 6.9 %collective-permute-start.1 = (bf16[2,256]{1,0:T(2,128)(2,1)}, bf16[2,256]{1,0:T(2,128)(2,1)S(1)}, u32[]{:S(2)}, u32[]{:S(2)}) collective-permute-start(bf16[2,256]{1,0:T(2,128)(2,1)} %param.19), channel_id=1, source_target_pairs={{0,7},{1,6},{2,5},{3,4},{4,3},{5,2},{6,1},{7,0},{8,14},{9,15},{10,... | collective-permute-start | bytes 3080 | tf_op jit(solution)/shard_map/ppermute | solution.py:369
  7.2 4.4 %copy-start.1 = (bf16[2,256]{1,0:T(2,128)(2,1)S(1)}, bf16[2,256]{1,0:T(2,128)(2,1)}, u32[]{:S(2)}) copy-start(bf16[2,256]{1,0:T(2,128)(2,1)} %param.19) | copy-start | bytes 3076
  7.2 8.7 %copy-start = (bf16[9,256,256]{2,1,0:T(8,128)(2,1)S(1)}, bf16[9,256,256]{2,1,0:T(8,128)(2,1)}, u32[]{:S(2)}) copy-start(bf16[9,256,256]{2,1,0:T(8,128)(2,1)} %r_4_.1) | copy-start | bytes 3538948
  11.7 4.1 %collective-permute-start.4 = (bf16[32,384]{1,0:T(8,128)(2,1)S(1)}, bf16[32,384]{1,0:T(8,128)(2,1)S(1)}, u32[]{:S(2)}, u32[]{:S(2)}) collective-permute-start(bf16[32,384]{1,0:T(8,128)(2,1)S(1)} %pad_maximum_fusion.r_0_), channel_id=1, source_target_pairs={{0,16},{8,24},{16,0},{24,8},{1,17},{9,25},{17,1},{25,9},{2,18},{10... | collective-permute-start | bytes 73736 | tf_op jit(solution)/shard_map/ppermute | solution.py:204
  12.3 3.5 %collective-permute-start.3 = (bf16[32,384]{1,0:T(8,128)(2,1)S(1)}, bf16[32,384]{1,0:T(8,128)(2,1)S(1)}, u32[]{:S(2)}, u32[]{:S(2)}) collective-permute-start(bf16[32,384]{1,0:T(8,128)(2,1)S(1)} %pad_maximum_fusion.r_0_), channel_id=1, source_target_pairs={{0,24},{8,16},{16,8},{24,0},{1,25},{9,17},{17,9},{25,1},{2,26},{10... | collective-permute-start | bytes 73736 | tf_op jit(solution)/shard_map/ppermute | solution.py:204
  12.3 3.5 %collective-permute-start.2 = (bf16[32,384]{1,0:T(8,128)(2,1)S(1)}, bf16[32,384]{1,0:T(8,128)(2,1)S(1)}, u32[]{:S(2)}, u32[]{:S(2)}) collective-permute-start(bf16[32,384]{1,0:T(8,128)(2,1)S(1)} %pad_maximum_fusion.r_0_), channel_id=1, source_target_pairs={{0,8},{8,0},{16,24},{24,16},{1,9},{9,1},{17,25},{25,17},{2,10},{10... | collective-permute-start | bytes 73736 | tf_op jit(solution)/shard_map/ppermute | solution.py:204
  17.3 3.6 %collective-permute-start.6 = (bf16[80,256]{1,0:T(8,128)(2,1)S(1)}, bf16[80,256]{1,0:T(8,128)(2,1)S(1)}, u32[]{:S(2)}, u32[]{:S(2)}) collective-permute-start(bf16[80,256]{1,0:T(8,128)(2,1)S(1)} %get-tuple-element.6.r_0_), channel_id=1, source_target_pairs={{0,24},{8,16},{16,8},{24,0},{1,25},{9,17},{17,9},{25,1},{2,26},{10... | collective-permute-start | bytes 122888 | tf_op jit(solution)/shard_map/ppermute | solution.py:204
  21.4 4.0 %collective-permute-start.7 = (f32[8,384]{1,0:T(8,128)S(1)}, f32[8,384]{1,0:T(8,128)S(1)}, u32[]{:S(2)}, u32[]{:S(2)}) collective-permute-start(f32[8,384]{1,0:T(8,128)S(1)} %slice.28), channel_id=1, source_target_pairs={{0,12},{1,13},{2,14},{3,15},{4,8},{5,9},{6,10},{7,11},{8,4},{9,5},... | collective-permute-start | bytes 36872 | tf_op jit(solution)/shard_map/ppermute | solution.py:199
  25.4 3.1 %collective-permute-start.8 = (f32[4,384]{1,0:T(4,128)S(1)}, f32[4,384]{1,0:T(4,128)S(1)}, u32[]{:S(2)}, u32[]{:S(2)}) collective-permute-start(f32[4,384]{1,0:T(4,128)S(1)} %slice.37), channel_id=1, source_target_pairs={{0,10},{1,11},{2,8},{3,9},{4,14},{5,15},{6,12},{7,13},{8,2},{9,3},... | collective-permute-start | bytes 18440 | tf_op jit(solution)/shard_map/ppermute | solution.py:199
  28.6 3.1 %collective-permute-start.9 = (f32[2,384]{1,0:T(2,128)S(1)}, f32[2,384]{1,0:T(2,128)S(1)}, u32[]{:S(2)}, u32[]{:S(2)}) collective-permute-start(f32[2,384]{1,0:T(2,128)S(1)} %slice.39), channel_id=1, source_target_pairs={{0,9},{1,8},{2,11},{3,10},{4,13},{5,12},{6,15},{7,14},{8,1},{9,0},... | collective-permute-start | bytes 9224 | tf_op jit(solution)/shard_map/ppermute | solution.py:199

commit v5 on v3

--- a/solution.py
+++ b/solution.py
@@ -389,11 +389,14 @@
     )
     refs = jnp.pad(refs, ((0, -refs.shape[0] % 16), (0, message.shape[1] - width)))
     message = jnp.concatenate([message, refs], axis=0)
+    others = {k: swap(message, "section", k) for k in range(1, sections, 2)}
+    for k in range(2, sections, 2):
+        others[k] = swap(others[k ^ 1], "section", 1)
     marg, listed = small_call(
         lambda *r: score_kernel(particles, sections, own_classes, classes, *r),
         "scores",
         message,
-        *[swap(message, "section", k) for k in range(1, sections)],
+        *[others[k] for k in range(1, sections)],
         rotations,
         sibling_rotations,
         out_shape=(

time: 32.3 us -> 32.7 us (1.012)
  waiting for transfers between devices: 12 us -> 13.9 us
  starting transfers between devices: 11.9 us -> 10.4 us
    ppermute x5, waiting for transfers between devices: 5.11 us -> 6.76 us  [swap(): return lax.ppermute(array, axis, [(i, i ^ distance) for i in range(size)])]
    ppermute x5, starting transfers between devices: 2.97 us -> 1.86 us  [swap(): return lax.ppermute(array, axis, [(i, i ^ distance) for i in range(size)])]
    ppermute x3, starting transfers between devices: 2.93 us -> 2.55 us  [cross(): return lax.ppermute(array, ('section', 'cls'), pairs)]
where the time goes in v5:
time: 32.7 us; the launch traced here: 32.5 us
  waiting for transfers between devices  13.9 us (43%)
  starting transfers between devices  10.4 us (32%)
  Pallas kernels  6.29 us (19%)
  between operations  0.71 us (2%)
  other arithmetic  0.63 us (2%)
  local copies, waits for them, and re-layouts  0.54 us (2%)
    ppermute x3, waiting for transfers between devices, cross(): return lax.ppermute(array, ('section', 'cls'), pairs)  7.17 us
    ppermute x5, waiting for transfers between devices, swap(): return lax.ppermute(array, axis, [(i, i ^ distance) for i in range(size)])  6.76 us
    ppermute x2, starting transfers between devices, body(): block = lax.ppermute(references, ('section', 'cls'), pairs)  6.02 us
    pallas_call x1, Pallas kernels, filter_images(): pl.pallas_call(lambda *refs: filter_kernel(own_classes, classes, *refs),...  4.41 us
    ppermute x3, starting transfers between devices, cross(): return lax.ppermute(array, ('section', 'cls'), pairs)  2.55 us
    pallas_call x2, Pallas kernels, small_call(): pl.pallas_call(kernel, out_shape=out_shape, in_specs=[pl.BlockSpec(memory...  1.88 us
    ppermute x5, starting transfers between devices, swap(): return lax.ppermute(array, axis, [(i, i ^ distance) for i in range(size)])  1.86 us
  transfers between devices with their start and end apart: 10, of which 6 were waited for; matrix products, arithmetic and copies ran while one was open for 2% of the time, Pallas kernels for 14%

profile of v5, /device:TPU:0, one launch (start us, length us, event | category | flops | bytes accessed | tf_op | source)
XLA Modules:
  0.0 32.5 jit_solution(1837770201020248828)
XLA Ops:
  0.6 0.5 %collective-permute-start.5 = (bf16[9,256,256]{2,1,0:T(8,128)(2,1)}, bf16[9,256,256]{2,1,0:T(8,128)(2,1)S(1)}, u32[]{:S(2)}, u32[]{:S(2)}) collective-permute-start(bf16[9,256,256]{2,1,0:T(8,128)(2,1)} %r_4_.1), channel_id=1, source_target_pairs={{0,8},{8,0},{16,24},{24,16},{1,9},{9,1},{17,25},{25,17},{2,10},{10... | collective-permute-start | bytes 3538952 | tf_op jit(solution)/shard_map/ppermute | solution.py:204
  1.2 3.6 %collective-permute-start = (bf16[2,256]{1,0:T(2,128)(2,1)}, bf16[2,256]{1,0:T(2,128)(2,1)S(1)}, u32[]{:S(2)}, u32[]{:S(2)}) collective-permute-start(bf16[2,256]{1,0:T(2,128)(2,1)} %param.19), channel_id=1, source_target_pairs={{0,3},{1,2},{2,1},{3,0},{4,7},{5,6},{6,5},{7,4},{8,10},{9,11},{10,... | collective-permute-start | bytes 3080 | tf_op jit(solution)/shard_map/ppermute | solution.py:367
  4.8 2.4 %collective-permute-start.1 = (bf16[2,256]{1,0:T(2,128)(2,1)}, bf16[2,256]{1,0:T(2,128)(2,1)S(1)}, u32[]{:S(2)}, u32[]{:S(2)}) collective-permute-start(bf16[2,256]{1,0:T(2,128)(2,1)} %param.19), channel_id=1, source_target_pairs={{0,7},{1,6},{2,5},{3,4},{4,3},{5,2},{6,1},{7,0},{8,14},{9,15},{10,... | collective-permute-start | bytes 3080 | tf_op jit(solution)/shard_map/ppermute | solution.py:367
  7.2 4.4 %filter_images.1 = bf16[16,384]{1,0:T(8,128)(2,1)S(1)} custom-call(s32[16]{0:T(128)} %refs_0_.1, s32[16]{0:T(128)} %refs_1_.1, bf16[16,256,256]{2,1,0:T(8,128)(2,1)} %refs_2_.1, bf16[4,256,256]{2,1,0:T(8,128)(2,1)} %refs_3_.1, bf16[4,256,256]{2,1,0:T(8,128)(2,1)} %refs_4_.1, f32[256,256]{1,0:T(8,128)} %constant.14.clone.refs_5_, bf16[16,256]{1,0:T(8,128)(2,1)} %bitcast.5, ...), custom_call_target="tpu_custom_call" | custom-call | flops 1073741824 | bytes 3145728 | tf_op jit(solution)/shard_map/filter_images/pallas_call | solution.py:158
  11.6 0.0 collective-permute-done
  11.6 0.0 collective-permute-done.1
  11.7 0.2 collective-permute-start.3
  11.9 0.6 %collective-permute-start.2 = (bf16[32,384]{1,0:T(8,128)(2,1)S(1)}, bf16[32,384]{1,0:T(8,128)(2,1)S(1)}, u32[]{:S(2)}, u32[]{:S(2)}) collective-permute-start(bf16[32,384]{1,0:T(8,128)(2,1)S(1)} %pad_maximum_fusion.r_0_), channel_id=1, source_target_pairs={{0,8},{8,0},{16,24},{24,16},{1,9},{9,1},{17,25},{25,17},{2,10},{10... | collective-permute-start | bytes 73736 | tf_op jit(solution)/shard_map/ppermute | solution.py:204
  12.5 2.5 %collective-permute-done.3.r_3_ = bf16[32,384]{1,0:T(8,128)(2,1)S(1)} collective-permute-done((bf16[32,384]{1,0:T(8,128)(2,1)S(1)}, bf16[32,384]{1,0:T(8,128)(2,1)S(1)}, u32[]{:S(2)}, u32[]{:S(2)}) %collective-permute-start.3) | collective-permute-done | bytes 24608 | tf_op jit(solution)/shard_map/ppermute | solution.py:204
  15.0 0.0 collective-permute-start.4
  15.0 0.0 collective-permute-done.2.r_1_
  15.0 1.2 %collective-permute-done.4.r_2_ = bf16[32,384]{1,0:T(8,128)(2,1)S(1)} collective-permute-done((bf16[32,384]{1,0:T(8,128)(2,1)S(1)}, bf16[32,384]{1,0:T(8,128)(2,1)S(1)}, u32[]{:S(2)}, u32[]{:S(2)}) %collective-permute-start.4) | collective-permute-done | bytes 24608 | tf_op jit(solution)/shard_map/ppermute | solution.py:204
  16.2 1.5 %scores.1 = (bf16[80,256]{1,0:T(8,128)(2,1)S(1)}, f32[16,64]{1,0:T(8,128)S(1)}) custom-call(bf16[32,384]{1,0:T(8,128)(2,1)S(1)} %pad_maximum_fusion.r_0_, bf16[32,384]{1,0:T(8,128)(2,1)S(1)} %collective-permute-done.2.r_1_, bf16[32,384]{1,0:T(8,128)(2,1)S(1)} %collective-permute-done.4.r_2_, bf16[32,384]{1,0:T(8,128)(2,1)S(1)} %collective-permute-done.3.r_3_, ...), custom_call_target="tpu_custom_call" | custom-call | bytes 2457600 | tf_op jit(solution)/shard_map/scores/pallas_call | solution.py:327
  17.7 0.6 %collective-permute-start.6 = (bf16[80,256]{1,0:T(8,128)(2,1)S(1)}, bf16[80,256]{1,0:T(8,128)(2,1)S(1)}, u32[]{:S(2)}, u32[]{:S(2)}) collective-permute-start(bf16[80,256]{1,0:T(8,128)(2,1)S(1)} %get-tuple-element.6.r_0_), channel_id=1, source_target_pairs={{0,24},{8,16},{16,8},{24,0},{1,25},{9,17},{17,9},{25,1},{2,26},{10... | collective-permute-start | bytes 122888 | tf_op jit(solution)/shard_map/ppermute | solution.py:204
  18.2 3.0 %collective-permute-done.6.r_1_ = bf16[80,256]{1,0:T(8,128)(2,1)S(1)} collective-permute-done((bf16[80,256]{1,0:T(8,128)(2,1)S(1)}, bf16[80,256]{1,0:T(8,128)(2,1)S(1)}, u32[]{:S(2)}, u32[]{:S(2)}) %collective-permute-start.6) | collective-permute-done | bytes 40992 | tf_op jit(solution)/shard_map/ppermute | solution.py:204
  21.3 0.4 %class_sums.1 = (f32[16,384]{1,0:T(8,128)S(1)}, f32[1,64]{1,0:T(1,128)S(1)}) custom-call(bf16[80,256]{1,0:T(8,128)(2,1)S(1)} %get-tuple-element.6.r_0_, bf16[80,256]{1,0:T(8,128)(2,1)S(1)} %collective-permute-done.6.r_1_, f32[16,64]{1,0:T(8,128)S(1)} %get-tuple-element.7.r_2_), custom_call_target="tpu_custom_call" | custom-call | bytes 86016 | tf_op jit(solution)/shard_map/class_sums/pallas_call | solution.py:327
  21.7 0.4 %collective-permute-start.7 = (f32[8,384]{1,0:T(8,128)S(1)}, f32[8,384]{1,0:T(8,128)S(1)}, u32[]{:S(2)}, u32[]{:S(2)}) collective-permute-start(f32[8,384]{1,0:T(8,128)S(1)} %slice.28), channel_id=1, source_target_pairs={{0,12},{1,13},{2,14},{3,15},{4,8},{5,9},{6,10},{7,11},{8,4},{9,5},... | collective-permute-start | bytes 36872 | tf_op jit(solution)/shard_map/ppermute | solution.py:199
  22.0 3.7 %collective-permute-done.7 = f32[8,384]{1,0:T(8,128)S(1)} collective-permute-done((f32[8,384]{1,0:T(8,128)S(1)}, f32[8,384]{1,0:T(8,128)S(1)}, u32[]{:S(2)}, u32[]{:S(2)}) %collective-permute-start.7) | collective-permute-done | bytes 12320 | tf_op jit(solution)/shard_map/ppermute | solution.py:199
  25.7 0.7 %collective-permute-start.8 = (f32[4,384]{1,0:T(4,128)S(1)}, f32[4,384]{1,0:T(4,128)S(1)}, u32[]{:S(2)}, u32[]{:S(2)}) collective-permute-start(f32[4,384]{1,0:T(4,128)S(1)} %slice.37), channel_id=1, source_target_pairs={{0,10},{1,11},{2,8},{3,9},{4,14},{5,15},{6,12},{7,13},{8,2},{9,3},... | collective-permute-start | bytes 18440 | tf_op jit(solution)/shard_map/ppermute | solution.py:199
  26.4 2.4 %collective-permute-done.8 = f32[4,384]{1,0:T(4,128)S(1)} collective-permute-done((f32[4,384]{1,0:T(4,128)S(1)}, f32[4,384]{1,0:T(4,128)S(1)}, u32[]{:S(2)}, u32[]{:S(2)}) %collective-permute-start.8) | collective-permute-done | bytes 6176 | tf_op jit(solution)/shard_map/ppermute | solution.py:199
  28.9 1.5 %collective-permute-start.9 = (f32[2,384]{1,0:T(2,128)S(1)}, f32[2,384]{1,0:T(2,128)S(1)}, u32[]{:S(2)}, u32[]{:S(2)}) collective-permute-start(f32[2,384]{1,0:T(2,128)S(1)} %slice.39), channel_id=1, source_target_pairs={{0,9},{1,8},{2,11},{3,10},{4,13},{5,12},{6,15},{7,14},{8,1},{9,0},... | collective-permute-start | bytes 9224 | tf_op jit(solution)/shard_map/ppermute | solution.py:199
  30.3 0.5 %slice_bitcast_fusion = f32[16]{0:T(128)} fusion(f32[1,64]{1,0:T(1,128)S(1)} %get-tuple-element.9), kind=kLoop, calls=%fused_computation.16 | loop fusion | bytes 128 | tf_op jit(solution)/shard_map/squeeze | solution.py:427
  30.8 1.1 %collective-permute-done.9 = f32[2,384]{1,0:T(2,128)S(1)} collective-permute-done((f32[2,384]{1,0:T(2,128)S(1)}, f32[2,384]{1,0:T(2,128)S(1)}, u32[]{:S(2)}, u32[]{:S(2)}) %collective-permute-start.9) | collective-permute-done | bytes 3104 | tf_op jit(solution)/shard_map/ppermute | solution.py:199
  31.9 0.6 %fusion.6 = f32[2,256]{1,0:T(2,128)} fusion(f32[2,384]{1,0:T(2,128)S(1)} %slice_add_fusion.2, f32[2,128]{1,0:T(2,128)S(1)} %slice.41, bf16[2,256]{1,0:T(2,128)(2,1)S(1)} %copy-done.1), kind=kLoop, calls=%fused_computation.13 | loop fusion | flops 2560 | bytes 6144 | tf_op jit(solution)/shard_map/div | solution.py:426
  (15 shorter events, 0.1 us)
Async XLA Ops:
  0.6 15.6 %collective-permute-start.5 = (bf16[9,256,256]{2,1,0:T(8,128)(2,1)}, bf16[9,256,256]{2,1,0:T(8,128)(2,1)S(1)}, u32[]{:S(2)}, u32[]{:S(2)}) collective-permute-start(bf16[9,256,256]{2,1,0:T(8,128)(2,1)} %r_4_.1), channel_id=1, source_target_pairs={{0,8},{8,0},{16,24},{24,16},{1,9},{9,1},{17,25},{25,17},{2,10},{10... | collective-permute-start | bytes 3538952 | tf_op jit(solution)/shard_map/ppermute | solution.py:204
  1.2 10.5 %collective-permute-start = (bf16[2,256]{1,0:T(2,128)(2,1)}, bf16[2,256]{1,0:T(2,128)(2,1)S(1)}, u32[]{:S(2)}, u32[]{:S(2)}) collective-permute-start(bf16[2,256]{1,0:T(2,128)(2,1)} %param.19), channel_id=1, source_target_pairs={{0,3},{1,2},{2,1},{3,0},{4,7},{5,6},{6,5},{7,4},{8,10},{9,11},{10,... | collective-permute-start | bytes 3080 | tf_op jit(solution)/shard_map/ppermute | solution.py:367
  4.8 6.9 %collective-permute-start.1 = (bf16[2,256]{1,0:T(2,128)(2,1)}, bf16[2,256]{1,0:T(2,128)(2,1)S(1)}, u32[]{:S(2)}, u32[]{:S(2)}) collective-permute-start(bf16[2,256]{1,0:T(2,128)(2,1)} %param.19), channel_id=1, source_target_pairs={{0,7},{1,6},{2,5},{3,4},{4,3},{5,2},{6,1},{7,0},{8,14},{9,15},{10,... | collective-permute-start | bytes 3080 | tf_op jit(solution)/shard_map/ppermute | solution.py:367
  7.2 4.4 %copy-start.1 = (bf16[2,256]{1,0:T(2,128)(2,1)S(1)}, bf16[2,256]{1,0:T(2,128)(2,1)}, u32[]{:S(2)}) copy-start(bf16[2,256]{1,0:T(2,128)(2,1)} %param.19) | copy-start | bytes 3076
  7.2 9.0 %copy-start = (bf16[9,256,256]{2,1,0:T(8,128)(2,1)S(1)}, bf16[9,256,256]{2,1,0:T(8,128)(2,1)}, u32[]{:S(2)}) copy-start(bf16[9,256,256]{2,1,0:T(8,128)(2,1)} %r_4_.1) | copy-start | bytes 3538948
  11.7 3.3 %collective-permute-start.3 = (bf16[32,384]{1,0:T(8,128)(2,1)S(1)}, bf16[32,384]{1,0:T(8,128)(2,1)S(1)}, u32[]{:S(2)}, u32[]{:S(2)}) collective-permute-start(bf16[32,384]{1,0:T(8,128)(2,1)S(1)} %pad_maximum_fusion.r_0_), channel_id=1, source_target_pairs={{0,24},{8,16},{16,8},{24,0},{1,25},{9,17},{17,9},{25,1},{2,26},{10... | collective-permute-start | bytes 73736 | tf_op jit(solution)/shard_map/ppermute | solution.py:204
  11.9 3.1 %collective-permute-start.2 = (bf16[32,384]{1,0:T(8,128)(2,1)S(1)}, bf16[32,384]{1,0:T(8,128)(2,1)S(1)}, u32[]{:S(2)}, u32[]{:S(2)}) collective-permute-start(bf16[32,384]{1,0:T(8,128)(2,1)S(1)} %pad_maximum_fusion.r_0_), channel_id=1, source_target_pairs={{0,8},{8,0},{16,24},{24,16},{1,9},{9,1},{17,25},{25,17},{2,10},{10... | collective-permute-start | bytes 73736 | tf_op jit(solution)/shard_map/ppermute | solution.py:204
  15.0 1.2 %collective-permute-start.4 = (bf16[32,384]{1,0:T(8,128)(2,1)S(1)}, bf16[32,384]{1,0:T(8,128)(2,1)S(1)}, u32[]{:S(2)}, u32[]{:S(2)}) collective-permute-start(bf16[32,384]{1,0:T(8,128)(2,1)S(1)} %collective-permute-done.3.r_3_), channel_id=1, source_target_pairs={{0,8},{8,0},{16,24},{24,16},{1,9},{9,1},{17,25},{25,17},{2,10},{10... | collective-permute-start | bytes 73736 | tf_op jit(solution)/shard_map/ppermute | solution.py:204
  17.7 3.6 %collective-permute-start.6 = (bf16[80,256]{1,0:T(8,128)(2,1)S(1)}, bf16[80,256]{1,0:T(8,128)(2,1)S(1)}, u32[]{:S(2)}, u32[]{:S(2)}) collective-permute-start(bf16[80,256]{1,0:T(8,128)(2,1)S(1)} %get-tuple-element.6.r_0_), channel_id=1, source_target_pairs={{0,24},{8,16},{16,8},{24,0},{1,25},{9,17},{17,9},{25,1},{2,26},{10... | collective-permute-start | bytes 122888 | tf_op jit(solution)/shard_map/ppermute | solution.py:204
  21.7 4.0 %collective-permute-start.7 = (f32[8,384]{1,0:T(8,128)S(1)}, f32[8,384]{1,0:T(8,128)S(1)}, u32[]{:S(2)}, u32[]{:S(2)}) collective-permute-start(f32[8,384]{1,0:T(8,128)S(1)} %slice.28), channel_id=1, source_target_pairs={{0,12},{1,13},{2,14},{3,15},{4,8},{5,9},{6,10},{7,11},{8,4},{9,5},... | collective-permute-start | bytes 36872 | tf_op jit(solution)/shard_map/ppermute | solution.py:199
  25.7 3.1 %collective-permute-start.8 = (f32[4,384]{1,0:T(4,128)S(1)}, f32[4,384]{1,0:T(4,128)S(1)}, u32[]{:S(2)}, u32[]{:S(2)}) collective-permute-start(f32[4,384]{1,0:T(4,128)S(1)} %slice.37), channel_id=1, source_target_pairs={{0,10},{1,11},{2,8},{3,9},{4,14},{5,15},{6,12},{7,13},{8,2},{9,3},... | collective-permute-start | bytes 18440 | tf_op jit(solution)/shard_map/ppermute | solution.py:199
  28.9 3.1 %collective-permute-start.9 = (f32[2,384]{1,0:T(2,128)S(1)}, f32[2,384]{1,0:T(2,128)S(1)}, u32[]{:S(2)}, u32[]{:S(2)}) collective-permute-start(f32[2,384]{1,0:T(2,128)S(1)} %slice.39), channel_id=1, source_target_pairs={{0,9},{1,8},{2,11},{3,10},{4,13},{5,12},{6,15},{7,14},{8,1},{9,0},... | collective-permute-start | bytes 9224 | tf_op jit(solution)/shard_map/ppermute | solution.py:199
